TPU v7x, 32 devices: a whole 2x2x4 slice. The times are simulated.
32 devices in a mesh: dp: 2 (over core), expert: 16 (over z, y, x).
Axes of the slice: x: 2, y: 2, z: 4, core: 2. Of those that a mesh axis runs over, the one named last changes fastest.
Arguments:
- tokens: bfloat16 [32, 1024, 768], P(('dp', 'expert')), may hold values from -6 to 6
- lengths: int32 [32], P(('dp', 'expert')), may hold values from 1 to 1024, 24576 in all
- expert_ids: int32 [32, 1024, 1], P(('dp', 'expert')), may hold values from 0 to 15; in each aligned block of 1024 rows (0 to 1023, 1024 to 2047, ..., all dimensions but the last counted through in order) at most 96 rows name the same one
- w_qkv: bfloat16 [768, 2304], replicated, may hold values from -0.21875 to 0.21875
- w_out: bfloat16 [768, 768], replicated, may hold values from -1.75 to 1.75
- norm1_gain: float32 [768], replicated, may hold values from 0.5 to 1.5
- norm2_gain: float32 [768], replicated, may hold values from 0.5 to 1.5
- w_in: bfloat16 [16, 768, 3072], P('expert'), may hold values from -0.21875 to 0.21875
- w_back: bfloat16 [16, 3072, 768], P('expert'), may hold values from -0.25 to 0.25
- cotangent: bfloat16 [32, 1024, 768], P(('dp', 'expert')), may hold values from -6 to 6
Outputs:
- output: float32 [32, 1024, 768], P(('dp', 'expert'))
- tokens_grad: float32 [32, 1024, 768], P(('dp', 'expert'))
- w_qkv_grad: float32 [768, 2304], replicated
- w_out_grad: float32 [768, 768], replicated
- norm1_gain_grad: float32 [768], replicated
- norm2_gain_grad: float32 [768], replicated
- w_in_grad: float32 [16, 768, 3072], P('expert')
- w_back_grad: float32 [16, 3072, 768], P('expert')
Inputs may be any that keep to these rules, and one draw needn't show every extreme that they name: `lengths`: each sequence's live tokens are its first ones; the longest sequence fills all 1024 positions. `expert_ids`: among the 1024 positions of one sequence, padded ones included, no expert is named more than 96 times, and in some sequence one expert is named exactly 96 times.
All inputs are finite; a program needn't handle non-finite values. No bound on the sum of `lengths` on one device may be relied on, other than what follows from the above.
Results may differ from a plain program's by a relative error of at most 0.012.
Values may be sent and summed in bfloat16 or wider, within the bound.
A program may use at most 256 MiB of HBM per device.

v0:
```python
import jax
import jax.numpy as jnp
from jax import lax
from jax.sharding import PartitionSpec as P

HEADS = 12
HEAD = 64


epsilon = 1e-05


def normalize(values):
    center = values - jnp.mean(values, axis=-1, keepdims=True)
    variance = jnp.mean(center * center, axis=-1, keepdims=True)
    inverse = lax.rsqrt(variance + epsilon)
    return (center * inverse, inverse)


def norm_back(grad_hat, scaled, inverse):
    mean_grad = jnp.mean(grad_hat, axis=-1, keepdims=True)
    second = jnp.mean(grad_hat * scaled, axis=-1, keepdims=True)
    return inverse * (grad_hat - mean_grad - scaled * second)


def contract_rows(left, right):
    return lax.dot_general(
        left, right, (((0,), (0,)), ((), ())), preferred_element_type=jnp.float32
    )


def contract_cols(left, right):
    return lax.dot_general(
        left, right, (((1,), (1,)), ((), ())), preferred_element_type=jnp.float32
    )


def shards(
    tokens, lengths, expert_ids, w_qkv, w_out, norm1_gain, norm2_gain, w_in, w_back, cotangent
):
    input_tokens = tokens[0].astype(jnp.float32)
    seq_len, width = input_tokens.shape
    heads = HEADS
    head_dim = HEAD
    scale = head_dim ** (-0.5)
    block_rows = min(512, seq_len)
    blocks = seq_len // block_rows
    seq_length = lengths[0]
    scaled_one, inverse_one = normalize(input_tokens)
    normalized_rows = (scaled_one * norm1_gain).astype(jnp.bfloat16)
    projected_output = jnp.dot(normalized_rows, w_qkv, preferred_element_type=jnp.float32).astype(
        jnp.bfloat16
    )
    query_heads = projected_output[:, :width].reshape(seq_len, heads, head_dim)
    key_heads = projected_output[:, width : 2 * width].reshape(seq_len, heads, head_dim)
    value_heads = projected_output[:, 2 * width :].reshape(seq_len, heads, head_dim)
    block_starts = jnp.arange(blocks, dtype=jnp.int32) * block_rows
    query_blocks = query_heads.reshape(blocks, block_rows, heads, head_dim)

    def block_scores(query_block, block_start):
        scores = (
            jnp.einsum("qhd,khd->hqk", query_block, key_heads, preferred_element_type=jnp.float32)
            * scale
        )
        row_index = block_start + lax.broadcasted_iota(jnp.int32, scores.shape, 1)
        col_index = lax.broadcasted_iota(jnp.int32, scores.shape, 2)
        allowed = (col_index <= row_index) & (col_index < seq_length)
        return jnp.where(allowed, scores, -1e30)

    def forward_block(packed):
        query_block, block_start = packed
        scores = block_scores(query_block, block_start)
        row_max = jnp.max(scores, axis=-1, keepdims=True)
        exponent = jnp.exp(scores - row_max)
        row_total = jnp.sum(exponent, axis=-1, keepdims=True)
        attention_weights = (exponent / row_total).astype(jnp.bfloat16)
        mixed_block = jnp.einsum(
            "hqk,khd->qhd", attention_weights, value_heads, preferred_element_type=jnp.float32
        )
        return (mixed_block, row_max + jnp.log(row_total))

    mixed_blocks, log_totals = lax.map(forward_block, (query_blocks, block_starts))
    mixed_output = mixed_blocks.reshape(seq_len, width).astype(jnp.bfloat16)
    residual_stream = input_tokens + jnp.dot(
        mixed_output, w_out, preferred_element_type=jnp.float32
    )
    scaled_two, inverse_two = normalize(residual_stream)
    expert_in = (scaled_two * norm2_gain).astype(jnp.bfloat16)
    experts_total = lax.axis_size("expert")
    capacity = 3 * seq_len // (2 * experts_total)
    positions = jnp.arange(seq_len, dtype=jnp.int32)
    is_live = positions < seq_length
    owner_ids = expert_ids[0, :, 0]
    choose = (
        (owner_ids[:, None] == jnp.arange(experts_total, dtype=jnp.int32)[None, :])
        & is_live[:, None]
    ).astype(jnp.int32)
    running = jnp.cumsum(choose, axis=0, dtype=jnp.int32)
    ranking = jnp.sum(running * choose, axis=1, dtype=jnp.int32) - 1
    slot_index = jnp.where(is_live, owner_ids * capacity + ranking, experts_total * capacity)

    def place(token_rows):
        buffer = (
            jnp.zeros((experts_total * capacity + 1, width), token_rows.dtype)
            .at[slot_index]
            .set(token_rows)
        )
        return buffer[:-1].reshape(experts_total, capacity, width)

    def collect(buffer):
        flat = buffer.reshape(-1, width)
        padded = jnp.concatenate([flat, jnp.zeros((1, width), flat.dtype)], axis=0)
        return padded[slot_index]

    outgoing = place(expert_in)
    arriving = lax.all_to_all(outgoing, "expert", split_axis=0, concat_axis=0, tiled=True)
    arrived_rows = arriving.reshape(-1, width)
    hidden = jax.nn.silu(jnp.dot(arrived_rows, w_in[0], preferred_element_type=jnp.float32)).astype(
        jnp.bfloat16
    )
    outcome = (
        jnp.dot(hidden, w_back[0], preferred_element_type=jnp.float32)
        .astype(jnp.bfloat16)
        .reshape(arriving.shape),
    )
    returned_out = lax.all_to_all(outcome[-1], "expert", split_axis=0, concat_axis=0, tiled=True)
    output = residual_stream + collect(returned_out).astype(jnp.float32)
    grad_out = place(cotangent[0])
    grad_in, rows_in = (
        lax.all_to_all(grad_out, "expert", split_axis=0, concat_axis=0, tiled=True),
        lax.all_to_all(outgoing, "expert", split_axis=0, concat_axis=0, tiled=True),
    )
    token_rows = rows_in.reshape(-1, width)
    grad_rows = grad_in.reshape(-1, width)
    pre_act = jnp.dot(token_rows, w_in[0], preferred_element_type=jnp.float32)
    gate_sig = jax.nn.sigmoid(pre_act)
    hidden = (pre_act * gate_sig).astype(jnp.bfloat16)
    back_grad = contract_rows(hidden, grad_rows)
    hidden_grad = contract_cols(grad_rows, w_back[0])
    act_grad = (hidden_grad * gate_sig * (1.0 + pre_act * (1.0 - gate_sig))).astype(jnp.bfloat16)
    in_grad = contract_rows(token_rows, act_grad)
    row_grad = contract_cols(act_grad, w_in[0]).astype(jnp.bfloat16).reshape(rows_in.shape)
    in_sum, back_sum = (
        lax.psum(in_grad[None].astype(jnp.bfloat16), "dp").astype(jnp.float32),
        lax.psum(back_grad[None].astype(jnp.bfloat16), "dp").astype(jnp.float32),
    )
    returned_grad = lax.all_to_all(row_grad, "expert", split_axis=0, concat_axis=0, tiled=True)
    normed_grad = collect(returned_grad).astype(jnp.float32)
    gain_two_grad = jnp.sum(normed_grad * scaled_two, axis=0)
    residual_grad = cotangent[0].astype(jnp.float32) + norm_back(
        normed_grad * norm2_gain, scaled_two, inverse_two
    )
    residual_low = residual_grad.astype(jnp.bfloat16)
    out_weight_grad = contract_rows(mixed_output, residual_low)
    mixed_grad = contract_cols(residual_low, w_out).astype(jnp.bfloat16)
    grad_blocks = mixed_grad.reshape(blocks, block_rows, heads, head_dim)

    def backward_block(carry, packed):
        key_grad, value_grad = carry
        query_block, out_grad_block, log_block, block_start = packed
        scores = block_scores(query_block, block_start)
        attention_probs = jnp.exp(scores - log_block)
        prob_grad = jnp.einsum(
            "qhd,khd->hqk", out_grad_block, value_heads, preferred_element_type=jnp.float32
        )
        inner = jnp.sum(attention_probs * prob_grad, axis=-1, keepdims=True)
        score_grad = (attention_probs * (prob_grad - inner)).astype(jnp.bfloat16)
        query_grad = (
            jnp.einsum("hqk,khd->qhd", score_grad, key_heads, preferred_element_type=jnp.float32)
            * scale
        )
        key_grad = (
            key_grad
            + jnp.einsum(
                "hqk,qhd->khd", score_grad, query_block, preferred_element_type=jnp.float32
            )
            * scale
        )
        value_grad = value_grad + jnp.einsum(
            "hqk,qhd->khd",
            attention_probs.astype(jnp.bfloat16),
            out_grad_block,
            preferred_element_type=jnp.float32,
        )
        return ((key_grad, value_grad), query_grad)

    zero_heads = jnp.zeros((seq_len, heads, head_dim), jnp.float32)
    (key_grad, value_grad), query_grad = lax.scan(
        backward_block,
        (zero_heads, zero_heads),
        (query_blocks, grad_blocks, log_totals, block_starts),
    )
    projected_grad = jnp.concatenate(
        [
            query_grad.reshape(seq_len, width),
            key_grad.reshape(seq_len, width),
            value_grad.reshape(seq_len, width),
        ],
        axis=1,
    ).astype(jnp.bfloat16)
    qkv_weight_grad = contract_rows(normalized_rows, projected_grad)
    normed_one_grad = contract_cols(projected_grad, w_qkv)
    gain_one_grad = jnp.sum(normed_one_grad * scaled_one, axis=0)
    input_grad = residual_grad + norm_back(normed_one_grad * norm1_gain, scaled_one, inverse_one)
    qkv_sum, out_sum, gain_one_sum, gain_two_sum = lax.psum(
        (qkv_weight_grad, out_weight_grad, gain_one_grad, gain_two_grad), ("dp", "expert")
    )
    return (
        output[None],
        input_grad[None],
        qkv_sum,
        out_sum,
        gain_one_sum,
        gain_two_sum,
        in_sum,
        back_sum,
    )


def solution(mesh):
    return jax.shard_map(
        shards,
        mesh=mesh,
        in_specs=(
            P(("dp", "expert"), None, None),
            P(("dp", "expert")),
            P(("dp", "expert"), None, None),
            P(),
            P(),
            P(),
            P(),
            P("expert", None, None),
            P("expert", None, None),
            P(("dp", "expert"), None, None),
        ),
        out_specs=(
            P(("dp", "expert"), None, None),
            P(("dp", "expert"), None, None),
            P(),
            P(),
            P(),
            P(),
            P("expert", None, None),
            P("expert", None, None),
        ),
        check_vma=False,
    )
```

profile of v0, /device:TPU:0, one launch (start us, length us, event | category | flops | bytes accessed | tf_op | source)
XLA Modules:
  0.0 835.6 jit_solution(18242578437392350746)
XLA Ops:
  10.1 9.3 %reduce-window.6 = s32[16,8,128]{2,1,0:T(8,128)} reduce-window(s32[16,8,128]{2,1,0:T(8,128)} %fusion.83, s32[]{:T(128)} %constant.52.clone.1), window={size=1x1x128 pad=0_0x0_0x127_0}, to_apply=%region_6.7 | reduce-window | flops 2080768 | bytes 131076 | tf_op jit(solution)/shard_map/reduce-window
  53.1 81.0 %while.27 = (s32[]{:T(128)}, bf16[2,512,12,64]{1,3,2,0:T(8,128)(2,1)}, f32[2,12,512,1]{2,1,3,0:T(8,128)}, s32[2]{0:T(128)S(1)}, s32[]{:T(128)}, /*index=5*/bf16[...) while((s32[]{:T(128)}, ...), condition=%wide.region_5.6_spmd, body=%wide.region_2.5_spmd.sunk | while | flops 1723854336 | bytes 201183536 | solution.py:82
  55.1 12.6 %fusion.125 = (f32[12,512]{1,0:T(8,128)S(1)}, f32[12,512,1024]{2,1,0:T(8,128)}) fusion(s32[512]{0:T(512)S(1)} %iota_add_fusion.4, pred[1024]{0:T(1024)(128)(4,1)S(1)} %iota_compare_fusion.9, bf16[1024,12,64]{0,2,1:T(8,128)(2,1)} %get-tuple-element.419, bf16[2,512,12,64]{1,3,2,0:T(8,128)(2,1)} %get-tuple-element.418, s32[]{:T(128)S(6)} %copy.63), kind=kOutput, calls=%fused_computation.10.clone.1 | convolution fusion | flops 836757504 | bytes 27552772 | tf_op jit(solution)/shard_map/while/body/eval_jaxpr/qhd,khd->hqk/dot_general | solution.py:62
  67.7 12.7 %fusion.126 = f32[12,512]{1,0:T(8,128)S(1)} fusion(f32[12,512,1024]{2,1,0:T(8,128)} %get-tuple-element.380, f32[12,512]{1,0:T(8,128)S(1)} %get-tuple-element.381, s32[512]{0:T(512)S(1)} %iota_add_fusion.4, pred[1024]{0:T(1024)(128)(4,1)S(1)} %iota_compare_fusion.9), kind=kLoop, calls=%fused_computation.9.clone.1 | loop fusion | flops 37742592 | bytes 25218048 | tf_op jit(solution)/shard_map/while/body/eval_jaxpr/reduce_sum | solution.py:75
  95.5 12.6 %fusion.125 = (f32[12,512]{1,0:T(8,128)S(1)}, f32[12,512,1024]{2,1,0:T(8,128)}) fusion(s32[512]{0:T(512)S(1)} %iota_add_fusion.4, pred[1024]{0:T(1024)(128)(4,1)S(1)} %iota_compare_fusion.9, bf16[1024,12,64]{0,2,1:T(8,128)(2,1)} %get-tuple-element.419, bf16[2,512,12,64]{1,3,2,0:T(8,128)(2,1)} %get-tuple-element.418, s32[]{:T(128)S(6)} %copy.63), kind=kOutput, calls=%fused_computation.10.clone.1 | convolution fusion | flops 836757504 | bytes 27552772 | tf_op jit(solution)/shard_map/while/body/eval_jaxpr/qhd,khd->hqk/dot_general | solution.py:62
  108.1 12.7 %fusion.126 = f32[12,512]{1,0:T(8,128)S(1)} fusion(f32[12,512,1024]{2,1,0:T(8,128)} %get-tuple-element.380, f32[12,512]{1,0:T(8,128)S(1)} %get-tuple-element.381, s32[512]{0:T(512)S(1)} %iota_add_fusion.4, pred[1024]{0:T(1024)(128)(4,1)S(1)} %iota_compare_fusion.9), kind=kLoop, calls=%fused_computation.9.clone.1 | loop fusion | flops 37742592 | bytes 25218048 | tf_op jit(solution)/shard_map/while/body/eval_jaxpr/reduce_sum | solution.py:75
  176.6 36.6 %all-to-all-done = bf16[16,96,768]{2,1,0:T(8,128)(2,1)} async-done(((bf16[16,96,768]{2,1,0:T(8,128)(2,1)}), bf16[16,96,768]{2,1,0:T(8,128)(2,1)}, u32[]{:S(2)}, u32[]{:S(2)}) %all-to-all-start) | async-done | bytes 2359328 | tf_op jit(solution)/shard_map/all_to_all | solution.py:116
  213.2 11.0 %all-to-all-start.2 = ((bf16[16,96,768]{2,1,0:T(8,128)(2,1)}), bf16[16,96,768]{2,1,0:T(8,128)(2,1)}, u32[]{:S(2)}, u32[]{:S(2)}) async-start(bf16[16,96,768]{2,1,0:T(8,128)(2,1)} %bitcast.216), calls=%async_computation.2 | async-start | bytes 4718592 | tf_op jit(solution)/shard_map/all_to_all | solution.py:130
  224.3 15.5 %multiply_convert_fusion.2 = (bf16[1536,3072]{1,0:T(8,128)(2,1)S(1)}, f32[1536,3072]{1,0:T(8,128)}) fusion(bf16[1536,768]{1,0:T(8,128)(2,1)} %bitcast.17, bf16[1,768,3072]{2,1,0:T(8,128)(2,1)} %param.21), kind=kOutput, calls=%fused_computation.49 | convolution fusion | flops 7271350272 | bytes 35389440 | tf_op jit(solution)/shard_map/dot_general | solution.py:118
  243.5 11.0 %fusion.51 = bf16[1536,768]{1,0:T(8,128)(2,1)} fusion(bf16[1536,3072]{1,0:T(8,128)(2,1)S(1)} %get-tuple-element.266, bf16[1,3072,768]{2,1,0:T(8,128)(2,1)} %param.22), kind=kOutput, calls=%fused_computation.80 | convolution fusion | flops 7248936960 | bytes 16515072 | tf_op jit(solution)/shard_map/dot_general | solution.py:122
  254.5 16.8 %all-to-all-done.2 = bf16[16,96,768]{2,1,0:T(8,128)(2,1)} async-done(((bf16[16,96,768]{2,1,0:T(8,128)(2,1)}), bf16[16,96,768]{2,1,0:T(8,128)(2,1)}, u32[]{:S(2)}, u32[]{:S(2)}) %all-to-all-start.2) | async-done | bytes 2359328 | tf_op jit(solution)/shard_map/all_to_all | solution.py:130
  271.4 11.0 %all-to-all-start.1 = ((bf16[16,96,768]{2,1,0:T(8,128)(2,1)}), bf16[16,96,768]{2,1,0:T(8,128)(2,1)}, u32[]{:S(2)}, u32[]{:S(2)}) async-start(bf16[16,96,768]{2,1,0:T(8,128)(2,1)} %bitcast.221), calls=%async_computation.1 | async-start | bytes 4718592 | tf_op jit(solution)/shard_map/all_to_all | solution.py:126
  282.4 19.1 %multiply_convert_fusion.1 = bf16[1536,3072]{1,0:T(8,128)(2,1)} fusion(f32[1536,3072]{1,0:T(8,128)} %get-tuple-element.267, bf16[1536,768]{1,0:T(8,128)(2,1)} %bitcast.26, bf16[1,3072,768]{2,1,0:T(8,128)(2,1)} %param.22), kind=kOutput, calls=%fused_computation.48 | convolution fusion | flops 7290224640 | bytes 35389440 | tf_op jit(solution)/shard_map/dot_general | solution.py:33
  301.5 12.5 %fusion.48 = bf16[1536,768]{1,0:T(8,128)(2,1)} fusion(bf16[1536,3072]{1,0:T(8,128)(2,1)} %multiply_convert_fusion.1, bf16[1,768,3072]{2,1,0:T(8,128)(2,1)} %param.21), kind=kOutput, calls=%fused_computation.79 | convolution fusion | flops 7248936960 | bytes 16515072 | tf_op jit(solution)/shard_map/dot_general | solution.py:33
  314.0 15.3 %all-to-all-done.1 = bf16[16,96,768]{2,1,0:T(8,128)(2,1)} async-done(((bf16[16,96,768]{2,1,0:T(8,128)(2,1)}), bf16[16,96,768]{2,1,0:T(8,128)(2,1)}, u32[]{:S(2)}, u32[]{:S(2)}) %all-to-all-start.1) | async-done | bytes 2359328 | tf_op jit(solution)/shard_map/all_to_all | solution.py:126
  329.4 10.8 %all-to-all-start.3 = ((bf16[16,96,768]{2,1,0:T(8,128)(2,1)}), bf16[16,96,768]{2,1,0:T(8,128)(2,1)}, u32[]{:S(2)}, u32[]{:S(2)}) async-start(bf16[16,96,768]{2,1,0:T(8,128)(2,1)} %bitcast.220), calls=%async_computation.3 | async-start | bytes 4718592 | tf_op jit(solution)/shard_map/all_to_all | solution.py:147
  343.7 12.3 %fusion.35 = bf16[1,768,3072]{2,1,0:T(8,128)(2,1)} fusion(bf16[1536,768]{1,0:T(8,128)(2,1)} %bitcast.17, bf16[1536,3072]{1,0:T(8,128)(2,1)} %multiply_convert_fusion.1), kind=kOutput, calls=%fused_computation.62 | convolution fusion | flops 7250116608 | bytes 16515072 | tf_op jit(solution)/shard_map/dot_general | solution.py:27
  356.1 12.3 %fusion.36 = bf16[1,3072,768]{2,1,0:T(8,128)(2,1)} fusion(bf16[1536,3072]{1,0:T(8,128)(2,1)} %copy-done.39, bf16[1536,768]{1,0:T(8,128)(2,1)} %bitcast.26), kind=kOutput, calls=%fused_computation.63 | convolution fusion | flops 7250116608 | bytes 16515072 | tf_op jit(solution)/shard_map/dot_general | solution.py:27
  426.6 178.5 %while.28 = (s32[]{:T(128)}, f32[1024,12,64]{0,2,1:T(8,128)}, f32[1024,12,64]{0,2,1:T(8,128)}, bf16[2,512,12,64]{1,3,2,0:T(8,128)(2,1)}, bf16[2,512,12,64]{1,3,2...) while((s32[]{:T(128)}, f32[1024,12,64]{0,2,1:T(8,128)}, ...), condition=%wide.region_17.18_spmd.clone, body=%wide.region_15.17_spmd.clone.sunk | while | flops 4100058624 | bytes 217192656 | solution.py:188
  430.1 13.4 %fusion.136 = f32[12,512,1024]{2,1,0:T(8,128)} fusion(bf16[1024,12,64]{0,2,1:T(8,128)(2,1)} %get-tuple-element.458, bf16[2,512,12,64]{1,3,2,0:T(8,128)(2,1)} %get-tuple-element.457, s32[]{:T(128)S(6)} %copy.73), kind=kOutput, calls=%fused_computation.33.clone.1 | convolution fusion | flops 805306368 | bytes 27525124 | tf_op jit(solution)/shard_map/while/body/eval_jaxpr/qhd,khd->hqk/dot_general | solution.py:163
  443.6 19.2 %multiply_reduce_fusion.4 = (f32[12,512]{1,0:T(8,128)}, f32[12,512,1024]{2,1,0:T(8,128)}) fusion(f32[12,512,1024]{2,1,0:T(8,128)} %fusion.136, f32[12,512]{1,0:T(8,128)} %dynamic-slice_bitcast_fusion.2, bf16[1024,12,64]{0,2,1:T(8,128)(2,1)} %get-tuple-element.455, bf16[2,512,12,64]{1,3,2,0:T(8,128)(2,1)} %get-tuple-element.452, s32[]{:T(128)S(6)} %copy.73, ...), kind=kOutput, calls=%fused_computation.23.clone.1 | convolution fusion | flops 849340416 | bytes 52751364 | tf_op jit(solution)/shard_map/while/body/eval_jaxpr/qhd,khd->hqk/dot_general | solution.py:62
  462.8 21.3 %multiply_convert_fusion.5 = bf16[12,512,1024]{2,1,0:T(8,128)(2,1)} fusion(f32[12,512,1024]{2,1,0:T(8,128)} %get-tuple-element.393, f32[12,512,1024]{2,1,0:T(8,128)} %fusion.136, f32[12,512]{1,0:T(8,128)} %get-tuple-element.394), kind=kLoop, calls=%fused_computation.22.clone.1 | loop fusion | flops 18874368 | bytes 62939136 | tf_op jit(solution)/shard_map/while/body/eval_jaxpr/convert_element_type | solution.py:167
  484.1 12.2 %bitcast_add_fusion.6 = f32[1024,12,64]{0,2,1:T(8,128)} fusion(f32[1024,12,64]{0,2,1:T(8,128)} %get-tuple-element.437, f32[12,512,1024]{2,1,0:T(8,128)} %get-tuple-element.393, pred[]{:T(512)S(6)} %compare.5, bf16[2,512,12,64]{1,3,2,0:T(8,128)(2,1)S(1)} %copy-done.4, s32[]{:T(128)S(6)} %copy.73), kind=kOutput, calls=%fused_computation.29.clone.1 | convolution fusion | flops 813170688 | bytes 32243716 | tf_op jit(solution)/shard_map/while/body/eval_jaxpr/hqk,qhd->khd/dot_general | solution.py:179
  496.3 9.8 %bitcast_dynamic-update-slice_fusion.8 = bf16[2,512,12,64]{1,3,2,0:T(8,128)(2,1)} fusion(bf16[2,512,12,64]{1,3,2,0:T(8,128)(2,1)} %get-tuple-element.438, s32[]{:T(128)S(6)} %copy.73, bf16[12,512,1024]{2,1,0:T(8,128)(2,1)} %multiply_convert_fusion.5, bf16[1024,12,64]{0,2,1:T(8,128)(2,1)} %get-tuple-element.455), kind=kOutput, calls=%fused_computation.31.clone.1 | convolution fusion | flops 805699584 | bytes 15728644 | tf_op jit(solution)/shard_map/while/body/eval_jaxpr/hqk,khd->qhd/dot_general | solution.py:169
  518.3 13.4 %fusion.136 = f32[12,512,1024]{2,1,0:T(8,128)} fusion(bf16[1024,12,64]{0,2,1:T(8,128)(2,1)} %get-tuple-element.458, bf16[2,512,12,64]{1,3,2,0:T(8,128)(2,1)} %get-tuple-element.457, s32[]{:T(128)S(6)} %copy.73), kind=kOutput, calls=%fused_computation.33.clone.1 | convolution fusion | flops 805306368 | bytes 27525124 | tf_op jit(solution)/shard_map/while/body/eval_jaxpr/qhd,khd->hqk/dot_general | solution.py:163
  531.7 19.2 %multiply_reduce_fusion.4 = (f32[12,512]{1,0:T(8,128)}, f32[12,512,1024]{2,1,0:T(8,128)}) fusion(f32[12,512,1024]{2,1,0:T(8,128)} %fusion.136, f32[12,512]{1,0:T(8,128)} %dynamic-slice_bitcast_fusion.2, bf16[1024,12,64]{0,2,1:T(8,128)(2,1)} %get-tuple-element.455, bf16[2,512,12,64]{1,3,2,0:T(8,128)(2,1)} %get-tuple-element.452, s32[]{:T(128)S(6)} %copy.73, ...), kind=kOutput, calls=%fused_computation.23.clone.1 | convolution fusion | flops 849340416 | bytes 52751364 | tf_op jit(solution)/shard_map/while/body/eval_jaxpr/qhd,khd->hqk/dot_general | solution.py:62
  551.0 21.3 %multiply_convert_fusion.5 = bf16[12,512,1024]{2,1,0:T(8,128)(2,1)} fusion(f32[12,512,1024]{2,1,0:T(8,128)} %get-tuple-element.393, f32[12,512,1024]{2,1,0:T(8,128)} %fusion.136, f32[12,512]{1,0:T(8,128)} %get-tuple-element.394), kind=kLoop, calls=%fused_computation.22.clone.1 | loop fusion | flops 18874368 | bytes 62939136 | tf_op jit(solution)/shard_map/while/body/eval_jaxpr/convert_element_type | solution.py:167
  572.3 13.1 %bitcast_add_fusion.6 = f32[1024,12,64]{0,2,1:T(8,128)} fusion(f32[1024,12,64]{0,2,1:T(8,128)} %get-tuple-element.437, f32[12,512,1024]{2,1,0:T(8,128)} %get-tuple-element.393, pred[]{:T(512)S(6)} %compare.5, bf16[2,512,12,64]{1,3,2,0:T(8,128)(2,1)S(1)} %copy-done.4, s32[]{:T(128)S(6)} %copy.73), kind=kOutput, calls=%fused_computation.29.clone.1 | convolution fusion | flops 813170688 | bytes 32243716 | tf_op jit(solution)/shard_map/while/body/eval_jaxpr/hqk,qhd->khd/dot_general | solution.py:179
  585.4 9.8 %bitcast_dynamic-update-slice_fusion.8 = bf16[2,512,12,64]{1,3,2,0:T(8,128)(2,1)} fusion(bf16[2,512,12,64]{1,3,2,0:T(8,128)(2,1)} %get-tuple-element.438, s32[]{:T(128)S(6)} %copy.73, bf16[12,512,1024]{2,1,0:T(8,128)(2,1)} %multiply_convert_fusion.5, bf16[1024,12,64]{0,2,1:T(8,128)(2,1)} %get-tuple-element.455), kind=kOutput, calls=%fused_computation.31.clone.1 | convolution fusion | flops 805699584 | bytes 15728644 | tf_op jit(solution)/shard_map/while/body/eval_jaxpr/hqk,khd->qhd/dot_general | solution.py:169
  595.2 9.7 %bitcast_add_fusion.5 = f32[1024,12,64]{0,2,1:T(8,128)} fusion(f32[1024,12,64]{0,2,1:T(8,128)} %get-tuple-element.436, bf16[12,512,1024]{2,1,0:T(8,128)(2,1)} %multiply_convert_fusion.5, pred[]{:T(512)S(6)} %compare.5, bf16[2,512,12,64]{1,3,2,0:T(8,128)(2,1)} %get-tuple-element.452, s32[]{:T(128)S(6)} %copy.73), kind=kOutput, calls=%fused_computation.30.clone.1 | convolution fusion | flops 807665664 | bytes 19660804 | tf_op jit(solution)/shard_map/while/body/eval_jaxpr/hqk,qhd->khd/dot_general | solution.py:174
  640.1 48.9 %all-reduce.2 = (f32[768]{0:T(1024)}, f32[768]{0:T(1024)}) all-reduce(f32[768]{0:T(1024)S(1)} %get-tuple-element.207, f32[768]{0:T(1024)S(1)} %copy-done.32), channel_id=1, replica_groups=mesh['dp'=2,'expert'=16] {'dp','expert'}, use_global_device_ids=true, to_apply=%region_23.24 | all-reduce | flops 1536 | bytes 12288 | tf_op jit(solution)/shard_map/psum | solution.py:205
  701.0 119.4 %all-reduce.8.cloned.1.call-done = (f32[768,2304]{1,0:T(8,128)}, f32[768,768]{1,0:T(8,128)}) async-done(((f32[768,2304]{1,0:T(8,128)}, f32[768,768]{1,0:T(8,128)}), (f32[768,2304]{1,0:T(8,128)}, f32[768,768]{1,0:T(8,128)})) %all-reduce.8.cloned.1.call-update) | async-done | bytes 9437200 | tf_op jit(solution)/shard_map/psum | solution.py:205
  (193 shorter events, 243.8 us)
Async XLA Ops:
  7.2 23.4 %copy-start = (bf16[768,2304]{1,0:T(8,128)(2,1)S(1)}, bf16[768,2304]{1,0:T(8,128)(2,1)}, u32[]{:S(2)}) copy-start(bf16[768,2304]{1,0:T(8,128)(2,1)} %param.17) | copy-start | bytes 10616836
  24.3 6.3 copy-start.33
  28.7 6.3 copy-start.26
  30.6 4.4 copy-start.30
  48.8 4.3 copy-start.37
  55.0 25.4 %copy-start.3 = (bf16[1024,12,64]{0,2,1:T(8,128)(2,1)S(1)}, bf16[1024,12,64]{0,2,1:T(8,128)(2,1)}, u32[]{:S(2)}) copy-start(bf16[1024,12,64]{0,2,1:T(8,128)(2,1)} %get-tuple-element.420) | copy-start | bytes 4718596 | tf_op jit(solution)/shard_map/while
  55.0 25.4 %copy-start.15 = (bf16[2,512,12,64]{1,3,2,0:T(8,128)(2,1)S(1)}, bf16[2,512,12,64]{1,3,2,0:T(8,128)(2,1)}, u32[]{:S(2)}) copy-start(bf16[2,512,12,64]{1,3,2,0:T(8,128)(2,1)} %get-tuple-element.405) | copy-start | bytes 4718596 | tf_op jit(solution)/shard_map/while
  67.7 15.5 %copy-start.1 = (f32[12,512,1024]{2,1,0:T(8,128)S(1)}, f32[12,512,1024]{2,1,0:T(8,128)}, u32[]{:S(2)}) copy-start(f32[12,512,1024]{2,1,0:T(8,128)} %get-tuple-element.380) | copy-start | bytes 75497472 | tf_op jit(solution)/shard_map/while
  83.2 8.6 %copy-start.24 = (f32[2,12,512,1]{2,1,3,0:T(8,128)S(1)}, f32[2,12,512,1]{2,1,3,0:T(8,128)}, u32[]{:S(2)}) copy-start(f32[2,12,512,1]{2,1,3,0:T(8,128)} %get-tuple-element.406) | copy-start | bytes 147460 | tf_op jit(solution)/shard_map/while
  95.5 25.4 %copy-start.3 = (bf16[1024,12,64]{0,2,1:T(8,128)(2,1)S(1)}, bf16[1024,12,64]{0,2,1:T(8,128)(2,1)}, u32[]{:S(2)}) copy-start(bf16[1024,12,64]{0,2,1:T(8,128)(2,1)} %get-tuple-element.420) | copy-start | bytes 4718596 | tf_op jit(solution)/shard_map/while
  95.5 25.4 %copy-start.15 = (bf16[2,512,12,64]{1,3,2,0:T(8,128)(2,1)S(1)}, bf16[2,512,12,64]{1,3,2,0:T(8,128)(2,1)}, u32[]{:S(2)}) copy-start(bf16[2,512,12,64]{1,3,2,0:T(8,128)(2,1)} %get-tuple-element.405) | copy-start | bytes 4718596 | tf_op jit(solution)/shard_map/while
  108.1 15.5 %copy-start.1 = (f32[12,512,1024]{2,1,0:T(8,128)S(1)}, f32[12,512,1024]{2,1,0:T(8,128)}, u32[]{:S(2)}) copy-start(f32[12,512,1024]{2,1,0:T(8,128)} %get-tuple-element.380) | copy-start | bytes 75497472 | tf_op jit(solution)/shard_map/while
  123.6 8.6 %copy-start.24 = (f32[2,12,512,1]{2,1,3,0:T(8,128)S(1)}, f32[2,12,512,1]{2,1,3,0:T(8,128)}, u32[]{:S(2)}) copy-start(f32[2,12,512,1]{2,1,3,0:T(8,128)} %get-tuple-element.406) | copy-start | bytes 147460 | tf_op jit(solution)/shard_map/while
  157.2 56.0 %all-to-all-start = ((bf16[16,96,768]{2,1,0:T(8,128)(2,1)}), bf16[16,96,768]{2,1,0:T(8,128)(2,1)}, u32[]{:S(2)}, u32[]{:S(2)}) async-start(bf16[16,96,768]{2,1,0:T(8,128)(2,1)} %bitcast.217), calls=%async_computation | async-start | bytes 4718592 | tf_op jit(solution)/shard_map/all_to_all | solution.py:116
  213.2 58.1 %all-to-all-start.2 = ((bf16[16,96,768]{2,1,0:T(8,128)(2,1)}), bf16[16,96,768]{2,1,0:T(8,128)(2,1)}, u32[]{:S(2)}, u32[]{:S(2)}) async-start(bf16[16,96,768]{2,1,0:T(8,128)(2,1)} %bitcast.216), calls=%async_computation.2 | async-start | bytes 4718592 | tf_op jit(solution)/shard_map/all_to_all | solution.py:130
  271.4 58.0 %all-to-all-start.1 = ((bf16[16,96,768]{2,1,0:T(8,128)(2,1)}), bf16[16,96,768]{2,1,0:T(8,128)(2,1)}, u32[]{:S(2)}, u32[]{:S(2)}) async-start(bf16[16,96,768]{2,1,0:T(8,128)(2,1)} %bitcast.221), calls=%async_computation.1 | async-start | bytes 4718592 | tf_op jit(solution)/shard_map/all_to_all | solution.py:126
  329.4 57.9 %all-to-all-start.3 = ((bf16[16,96,768]{2,1,0:T(8,128)(2,1)}), bf16[16,96,768]{2,1,0:T(8,128)(2,1)}, u32[]{:S(2)}, u32[]{:S(2)}) async-start(bf16[16,96,768]{2,1,0:T(8,128)(2,1)} %bitcast.220), calls=%async_computation.3 | async-start | bytes 4718592 | tf_op jit(solution)/shard_map/all_to_all | solution.py:147
  340.2 348.8 %all-reduce.10.cloned.1.call-start = ((), (), s32[]{:S(2)}) async-start(), calls=%async_computation.5 | async-start | bytes 18874368 | tf_op jit(solution)/shard_map/psum | solution.py:144
  368.4 452.0 %all-reduce.8.cloned.1.call-start = ((), (), s32[]{:S(2)}) async-start(), calls=%async_computation.4 | async-start | bytes 18874368 | tf_op jit(solution)/shard_map/psum | solution.py:205
  400.8 5.1 copy-start.6
  400.8 5.1 copy-start.11
  405.8 7.4 copy-start.36
  422.3 4.3 copy-start.38
  462.8 21.3 %copy-start.4 = (bf16[2,512,12,64]{1,3,2,0:T(8,128)(2,1)S(1)}, bf16[2,512,12,64]{1,3,2,0:T(8,128)(2,1)}, u32[]{:S(2)}) copy-start(bf16[2,512,12,64]{1,3,2,0:T(8,128)(2,1)} %get-tuple-element.457) | copy-start | bytes 4718596 | tf_op jit(solution)/shard_map/while
  551.0 21.3 %copy-start.4 = (bf16[2,512,12,64]{1,3,2,0:T(8,128)(2,1)S(1)}, bf16[2,512,12,64]{1,3,2,0:T(8,128)(2,1)}, u32[]{:S(2)}) copy-start(bf16[2,512,12,64]{1,3,2,0:T(8,128)(2,1)} %get-tuple-element.457) | copy-start | bytes 4718596 | tf_op jit(solution)/shard_map/while
  608.7 7.3 copy-start.21
  609.0 7.0 copy-start.22
  609.0 4.1 copy-start.20
  626.5 7.4 copy-start.10
  626.5 7.4 copy-start.14
  689.0 7.5 copy-start.17
  820.4 6.6 copy-start.18
  (21 other events, 54.2 us)
Sparse Core Ops, SparseCore 0:
  368.5 42.0 all-reduce.9
  623.1 197.2 all-reduce.7
where the time goes:
time: 846 us; the launch traced here: 836 us
  matrix products  280 us (33%)
  waiting for transfers between devices  193 us (23%)
  local copies, waits for them, and re-layouts  132 us (16%)
  other arithmetic  123 us (15%)
  blocking collectives  48.9 us (6%)
  starting transfers between devices  41.9 us (5%)
  between operations  15.9 us (2%)
    psum x1, waiting for transfers between devices, shards(): lax.psum((qkv_weight_grad, out_weight_grad, gain_one_grad, gain_two_grad)...  119 us
    dot_general x4, matrix products, block_scores(): jnp.einsum('qhd,khd->hqk', query_block, key_heads, preferred_element_type...  63.8 us
    psum x1, blocking collectives, shards(): lax.psum((qkv_weight_grad, out_weight_grad, gain_one_grad, gain_two_grad)...  48.9 us
    convert_element_type x2, other arithmetic, backward_block(): score_grad = (attention_probs * (prob_grad - inner)).astype(jnp.bfloat16)  42.6 us
    dot_general x4, matrix products, contract_cols(): lax.dot_general(left, right, (((1,), (1,)), ((), ())), preferred_element_...  41.6 us
    all_to_all x1, waiting for transfers between devices, shards(): lax.all_to_all(outgoing, 'expert', split_axis=0, concat_axis=0, tiled=True)  36.6 us
    dot_general x4, matrix products, contract_rows(): lax.dot_general(left, right, (((0,), (0,)), ((), ())), preferred_element_...  34.4 us
    unnamed x75, local copies, waits for them, and re-layouts  31.9 us
  transfers between devices with their start and end apart: 6, of which 5 were waited for; matrix products, arithmetic and copies ran while one was open for 45% of the time, Pallas kernels for 0%

commit v1 on v0

v1 whole, which is shorter than its diff:
```python
import functools

import jax
import jax.numpy as jnp
from jax import lax
from jax.experimental import pallas as pl
from jax.experimental.pallas import tpu as pltpu
from jax.sharding import PartitionSpec as P

BF, F32, I32 = jnp.bfloat16, jnp.float32, jnp.int32
HEAD = 64
LANES = 128
ROWS = 256
EPS = 1e-5
NEG = -1e30
VMEM = pl.BlockSpec(memory_space=pltpu.VMEM)
SMEM = pl.BlockSpec(memory_space=pltpu.SMEM)
MIB = 2**20


def dot(a, b):
    return lax.dot_general(a, b, (((1,), (0,)), ((), ())), preferred_element_type=F32)


def dot_t(a, b):
    return lax.dot_general(a, b, (((1,), (1,)), ((), ())), preferred_element_type=F32)


def tdot(a, b):
    return lax.dot_general(a, b, (((0,), (0,)), ((), ())), preferred_element_type=F32)


def rows_of(i, n=ROWS):
    return pl.ds(pl.multiple_of(i * n, n), n)


def normalize(x):
    center = x - jnp.mean(x, axis=-1, keepdims=True)
    inverse = lax.rsqrt(jnp.mean(center * center, axis=-1, keepdims=True) + EPS)
    return center * inverse, inverse


def norm_back(u, hat, inverse):
    return inverse * (
        u - jnp.mean(u, axis=-1, keepdims=True) - hat * jnp.mean(u * hat, axis=-1, keepdims=True)
    )


def lane_iota(shape):
    return lax.broadcasted_iota(I32, shape, len(shape) - 1)


def split_parts(x):
    high = x.astype(BF)
    rest = x - high.astype(F32)
    middle = rest.astype(BF)
    low = (rest - middle.astype(F32)).astype(BF)
    return high, middle, low


def aug_of(x, one):
    high, middle, low = split_parts(x)
    lane = lane_iota(x.shape) % HEAD
    parts = jnp.where(
        lane == 0,
        -high.astype(F32),
        jnp.where(
            lane == 1,
            -middle.astype(F32),
            jnp.where(lane == 2, -low.astype(F32), jnp.where(lane == 3, one, 0.0)),
        ),
    )
    return parts.astype(BF)


def key_aug(seq, length):
    lane = lane_iota((seq, LANES)) % HEAD
    row = lax.broadcasted_iota(I32, (seq, LANES), 0)
    dead = jnp.where(row < length, 0.0, NEG)
    return jnp.where(lane < 3, 1.0, jnp.where(lane == 3, dead, 0.0)).astype(BF)


def forward_kernel(
    experts, capacity,
    len_ref, tok_ref, eid_row_ref, eid_col_ref, wqkv_ref, wout_ref, g1_ref, g2_ref,
    normed_ref, qkv_ref, mixed_ref, laug_ref, h_ref, slots_ref, slot_col_ref,
    kaug_ref, xin_ref, slot_row_ref,
):
    seq, width = tok_ref.shape
    blocks, pairs = seq // ROWS, width // LANES
    length = len_ref[0]

    @pl.loop(0, blocks)
    def _(i):
        hat, _ = normalize(tok_ref[rows_of(i), :].astype(F32))
        normed_ref[rows_of(i), :] = (hat * g1_ref[...]).astype(BF)

    @pl.loop(0, 3 * pairs // 2)
    def _(j):
        w = wqkv_ref[:, rows_of(j, 2 * LANES)]
        for i in range(blocks):
            r = slice(i * ROWS, (i + 1) * ROWS)
            out = dot(normed_ref[r, :], w).astype(BF)
            qkv_ref[2 * j, r, :] = out[:, :LANES]
            qkv_ref[2 * j + 1, r, :] = out[:, LANES:]

    kaug_ref[...] = key_aug(seq, length)
    first = lane_iota((1, LANES)) < HEAD
    scale = jnp.asarray(HEAD**-0.5, BF)

    @pl.loop(0, pairs)
    def _(p):
        qaug = jnp.where(lane_iota((ROWS, LANES)) % HEAD == 3, 1.0, 0.0).astype(BF)
        causal = lane_iota((ROWS, ROWS)) <= lax.broadcasted_iota(I32, (ROWS, ROWS), 0)
        one = jnp.ones((1, LANES), BF)
        for i in range(blocks):
            r = slice(i * ROWS, (i + 1) * ROWS)
            n = (i + 1) * ROWS
            q = qkv_ref[p, r, :] * scale
            k = qkv_ref[pairs + p, :n, :]
            v = qkv_ref[2 * pairs + p, :n, :]
            aug = kaug_ref[:n, :]
            outs, tops = [], []
            for head in range(2):
                mine = first if head == 0 else ~first
                s = dot_t(jnp.where(mine, q, qaug), jnp.where(mine, k, aug))
                last = jnp.where(causal, s[:, n - ROWS :], NEG)
                s = jnp.concatenate([s[:, : n - ROWS], last], axis=1) if i else last
                top = jnp.max(s, axis=1, keepdims=True)
                e = jnp.exp(s - top).astype(BF)
                outs.append(dot(e, jnp.where(mine, v, one)))
                tops.append(top)
            above = jnp.where(first, outs[0], outs[1])
            below = jnp.where(first, outs[1], outs[0])
            mixed_ref[r, rows_of(p, LANES)] = (above / pltpu.roll(below, HEAD, 1)).astype(BF)
            lse = jnp.where(first, tops[1], tops[0]) + jnp.log(below)
            laug_ref[p, r, :] = aug_of(lse, 1.0)

    @pl.loop(0, blocks)
    def _(i):
        r = rows_of(i)
        h = tok_ref[r, :].astype(F32) + dot(mixed_ref[r, :], wout_ref[...])
        h_ref[r, :] = h
        hat, _ = normalize(h)
        xin_ref[r, :] = (hat * g2_ref[...]).astype(BF)

    tri = jnp.where(
        lax.broadcasted_iota(I32, (seq, seq), 0) <= lane_iota((seq, seq)), 1.0, 0.0
    ).astype(BF)
    eid = eid_row_ref[...]
    live = lane_iota((1, seq)) < length
    pick = (lax.broadcasted_iota(I32, (experts, seq), 0) == eid) & live
    pick = jnp.where(pick, 1.0, 0.0)
    rank = jnp.sum(dot(pick.astype(BF), tri) * pick, axis=0, keepdims=True).astype(I32) - 1
    slot_row_ref[...] = jnp.where(live, eid * capacity + rank, experts * capacity)

    eid = eid_col_ref[...]
    live = lax.broadcasted_iota(I32, (seq, 1), 0) < length
    pick = (lane_iota((seq, LANES)) == eid) & live
    pick = jnp.where(pick, 1.0, 0.0)
    rank = jnp.sum(tdot(tri, pick.astype(BF)) * pick, axis=1, keepdims=True).astype(I32) - 1
    slot_col_ref[...] = jnp.where(live, eid * capacity + rank, experts * capacity)

    total = experts * capacity
    step = 4 * capacity

    @pl.loop(0, total // step)
    def _(c):
        place(slot_row_ref, xin_ref, slots_ref, c, step)


def place(slot_row_ref, src_ref, slots_ref, c, step):
    seq = src_ref.shape[0]
    index = lax.broadcasted_iota(I32, (step, seq), 0) + c * step
    onehot = jnp.where(index == slot_row_ref[...], 1.0, 0.0).astype(BF)
    slots_ref[rows_of(c, step), :] = dot(onehot, src_ref[...]).astype(BF)


def collect(slot_col_ref, ret_ref, r):
    total = ret_ref.shape[0]
    onehot = jnp.where(slot_col_ref[r, :] == lane_iota((ROWS, total)), 1.0, 0.0).astype(BF)
    return dot(onehot, ret_ref[...])


def place_kernel(experts, capacity, len_ref, eid_row_ref, cot_ref, slots_ref, slot_row_ref):
    seq, _ = cot_ref.shape
    length = len_ref[0]
    tri = jnp.where(
        lax.broadcasted_iota(I32, (seq, seq), 0) <= lane_iota((seq, seq)), 1.0, 0.0
    ).astype(BF)
    eid = eid_row_ref[...]
    live = lane_iota((1, seq)) < length
    pick = (lax.broadcasted_iota(I32, (experts, seq), 0) == eid) & live
    pick = jnp.where(pick, 1.0, 0.0)
    rank = jnp.sum(dot(pick.astype(BF), tri) * pick, axis=0, keepdims=True).astype(I32) - 1
    slot_row_ref[...] = jnp.where(live, eid * capacity + rank, experts * capacity)
    total = experts * capacity
    step = 4 * capacity

    @pl.loop(0, total // step)
    def _(c):
        place(slot_row_ref, cot_ref, slots_ref, c, step)


def collect_kernel(h_ref, slot_col_ref, ret_ref, out_ref):
    @pl.loop(0, h_ref.shape[0] // ROWS)
    def _(i):
        r = rows_of(i)
        out_ref[r, :] = h_ref[r, :] + collect(slot_col_ref, ret_ref, r)


def expert_kernel(x_ref, g_ref, win_ref, wback_ref, ffn_ref, ing_ref, wing_ref, wbg_ref, ffn_acc, ing_acc):
    t = pl.program_id(0)
    total = x_ref.shape[0]
    tile = win_ref.shape[1]
    blocks = 4
    size = total // blocks

    @pl.when(t == 0)
    def _():
        ffn_acc[...] = jnp.zeros_like(ffn_acc)
        ing_acc[...] = jnp.zeros_like(ing_acc)

    hidden_parts, act_parts = [], []
    for i in range(blocks):
        r = slice(i * size, (i + 1) * size)
        a = dot(x_ref[r, :], win_ref[...])
        gate = jax.nn.sigmoid(a)
        hidden = (a * gate).astype(BF)
        back = dot_t(g_ref[r, :], wback_ref[...])
        act = (back * gate * (1.0 + a * (1.0 - gate))).astype(BF)
        ffn_acc[r, :] += dot(hidden, wback_ref[...])
        ing_acc[r, :] += dot_t(act, win_ref[...])
        hidden_parts.append(hidden)
        act_parts.append(act)
    wing_ref[...] = tdot(x_ref[...], jnp.concatenate(act_parts, axis=0)).astype(BF)
    wbg_ref[...] = tdot(jnp.concatenate(hidden_parts, axis=0), g_ref[...]).astype(BF)

    @pl.when(t == pl.num_programs(0) - 1)
    def _():
        ffn_ref[...] = ffn_acc[...].astype(BF)
        ing_ref[...] = ing_acc[...].astype(BF)


def backward_kernel(
    len_ref, tok_ref, cot_ref, normed_ref, qkv_ref, mixed_ref, laug_ref, h_ref, ret_ref, slot_col_ref,
    wqkv_ref, wout_ref, g1_ref, g2_ref,
    tokg_ref, wqkvg_ref, woutg_ref, g1g_ref, g2g_ref,
    hgrad_ref, hg_ref, mg_ref, daug_ref, kaug_ref, dq_ref, qg_ref, normt_ref,
):
    seq, width = tok_ref.shape
    blocks, pairs = seq // ROWS, width // LANES
    g1g_ref[...] = jnp.zeros_like(g1g_ref)
    g2g_ref[...] = jnp.zeros_like(g2g_ref)
    first = lane_iota((1, LANES)) < HEAD

    @pl.loop(0, blocks)
    def _(i):
        r = rows_of(i)
        hat, inverse = normalize(h_ref[r, :])
        ing = collect(slot_col_ref, ret_ref, r)
        g2g_ref[...] += jnp.sum(ing * hat, axis=0, keepdims=True)
        grad = cot_ref[r, :].astype(F32) + norm_back(ing * g2_ref[...], hat, inverse)
        hgrad_ref[r, :] = grad
        low = grad.astype(BF)
        hg_ref[r, :] = low
        mg = dot_t(low, wout_ref[...]).astype(BF)
        for p in range(pairs):
            part = mg[:, p * LANES : (p + 1) * LANES]
            mg_ref[p, r, :] = part
            prod = part.astype(F32) * mixed_ref[r, p * LANES : (p + 1) * LANES].astype(F32)
            zero = jnp.zeros_like(prod)
            d0 = jnp.sum(jnp.where(first, prod, zero), axis=1, keepdims=True)
            d1 = jnp.sum(jnp.where(first, zero, prod), axis=1, keepdims=True)
            daug_ref[p, r, :] = aug_of(jnp.where(first, d1, d0), 0.0)
        normt_ref[:, r] = normed_ref[r, :].T

    woutg_ref[...] = tdot(mixed_ref[...], hg_ref[...]).astype(BF)
    kaug_ref[...] = key_aug(seq, len_ref[0])
    scale = jnp.asarray(HEAD**-0.5, BF)

    @pl.loop(0, pairs)
    def _(p):
        keep = lane_iota((ROWS, ROWS)) >= lax.broadcasted_iota(I32, (ROWS, ROWS), 0)
        vaug = jnp.where(lane_iota((ROWS, LANES)) % HEAD < 3, 1.0, 0.0).astype(BF)
        none = jnp.zeros((ROWS, LANES), BF)
        dq_ref[...] = jnp.zeros_like(dq_ref)
        for j in range(blocks):
            kr = slice(j * ROWS, (j + 1) * ROWS)
            qr = slice(j * ROWS, seq)
            q = qkv_ref[p, qr, :] * scale
            k = qkv_ref[pairs + p, kr, :]
            v = qkv_ref[2 * pairs + p, kr, :]
            do = mg_ref[p, qr, :]
            la, da = laug_ref[p, qr, :], daug_ref[p, qr, :]
            ka = kaug_ref[kr, :]
            dvs, dks, dss, kms = [], [], [], []
            for head in range(2):
                mine = first if head == 0 else ~first
                s = dot_t(jnp.where(mine, k, ka), jnp.where(mine, q, la))
                e = jnp.exp(s)
                start = jnp.where(keep, e[:, :ROWS], 0.0)
                e = jnp.concatenate([start, e[:, ROWS:]], axis=1) if j < blocks - 1 else start
                dp = dot_t(jnp.where(mine, v, vaug), jnp.where(mine, do, da))
                ds = (e * dp).astype(BF)
                dvs.append(dot(e.astype(BF), do))
                dks.append(dot(ds, q))
                dss.append(ds)
                kms.append(jnp.where(mine, k, none))
            qg_ref[kr, rows_of(2 * pairs + p, LANES)] = jnp.where(first, dvs[0], dvs[1]).astype(BF)
            qg_ref[kr, rows_of(pairs + p, LANES)] = jnp.where(first, dks[0], dks[1]).astype(BF)
            dq_ref[qr, :] += tdot(jnp.concatenate(dss, axis=0), jnp.concatenate(kms, axis=0))
        qg_ref[:, rows_of(p, LANES)] = (dq_ref[...] * HEAD**-0.5).astype(BF)

    @pl.loop(0, 3 * pairs // 2)
    def _(j):
        c = rows_of(j, 2 * LANES)
        wqkvg_ref[:, c] = dot(normt_ref[...], qg_ref[:, c]).astype(BF)

    @pl.loop(0, blocks)
    def _(i):
        r = rows_of(i)
        n1 = dot_t(qg_ref[r, :], wqkv_ref[...])
        hat, inverse = normalize(tok_ref[r, :].astype(F32))
        g1g_ref[...] += jnp.sum(n1 * hat, axis=0, keepdims=True)
        tokg_ref[r, :] = hgrad_ref[r, :] + norm_back(n1 * g1_ref[...], hat, inverse)


def params(mib, **kw):
    return pltpu.CompilerParams(vmem_limit_bytes=mib * MIB, **kw)


def sds(shape, dtype):
    return jax.ShapeDtypeStruct(shape, dtype)


def shards(experts, tokens, lengths, expert_ids, w_qkv, w_out, norm1_gain, norm2_gain, w_in, w_back, cotangent):
    x, g = tokens[0], cotangent[0]
    seq, width = x.shape
    pairs = width // LANES
    capacity = 3 * seq // (2 * experts)
    capacity = (capacity + 15) // 16 * 16
    total = experts * capacity
    eid_row = expert_ids.reshape(1, seq)
    eid_col = expert_ids[0]
    g1, g2 = norm1_gain.reshape(1, width), norm2_gain.reshape(1, width)
    ff = w_in.shape[2]

    g_slots, _ = pl.pallas_call(
        functools.partial(place_kernel, experts, capacity),
        out_shape=(sds((total, width), BF), sds((1, seq), I32)),
        in_specs=[SMEM, VMEM, VMEM],
        out_specs=(VMEM, VMEM),
        compiler_params=params(40),
        name="place_gradient",
    )(lengths, eid_row, g)
    g_in = exchange(g_slots, experts)

    normed, qkv, mixed, laug, h, x_slots, slot_col = pl.pallas_call(
        functools.partial(forward_kernel, experts, capacity),
        out_shape=(
            sds((seq, width), BF),
            sds((3 * pairs, seq, LANES), BF),
            sds((seq, width), BF),
            sds((pairs, seq, LANES), BF),
            sds((seq, width), F32),
            sds((total, width), BF),
            sds((seq, 1), I32),
        ),
        in_specs=[SMEM] + [VMEM] * 7,
        out_specs=(VMEM,) * 7,
        scratch_shapes=[
            pltpu.VMEM((seq, LANES), BF),
            pltpu.VMEM((seq, width), BF),
            pltpu.VMEM((1, seq), I32),
        ],
        compiler_params=params(58),
        cost_estimate=pl.CostEstimate(flops=40 * 10**9, bytes_accessed=24 * 10**6, transcendentals=0),
        name="attention_forward",
    )(lengths, x, eid_row, eid_col, w_qkv, w_out, g1, g2)
    x_in = exchange(x_slots, experts)

    tile = 512
    full = pl.BlockSpec((total, width), lambda t: (0, 0))
    ffn, ing, wing, wbg = pl.pallas_call(
        expert_kernel,
        grid=(ff // tile,),
        out_shape=(
            sds((total, width), BF),
            sds((total, width), BF),
            sds((width, ff), BF),
            sds((ff, width), BF),
        ),
        in_specs=[
            full,
            full,
            pl.BlockSpec((width, tile), lambda t: (0, t)),
            pl.BlockSpec((tile, width), lambda t: (t, 0)),
        ],
        out_specs=(
            full,
            full,
            pl.BlockSpec((width, tile), lambda t: (0, t)),
            pl.BlockSpec((tile, width), lambda t: (t, 0)),
        ),
        scratch_shapes=[pltpu.VMEM((total, width), F32)] * 2,
        compiler_params=params(58),
        cost_estimate=pl.CostEstimate(flops=44 * 10**9, bytes_accessed=30 * 10**6, transcendentals=0),
        name="experts",
    )(x_in, g_in, w_in[0], w_back[0])
    ing_ret = exchange(ing, experts)
    ffn_ret = exchange(ffn, experts)

    tokg, wqkvg, woutg, g1g, g2g = pl.pallas_call(
        backward_kernel,
        out_shape=(
            sds((seq, width), F32),
            sds((width, 3 * width), BF),
            sds((width, width), BF),
            sds((1, width), F32),
            sds((1, width), F32),
        ),
        in_specs=[SMEM] + [VMEM] * 13,
        out_specs=(VMEM,) * 5,
        scratch_shapes=[
            pltpu.VMEM((seq, width), F32),
            pltpu.VMEM((seq, width), BF),
            pltpu.VMEM((pairs, seq, LANES), BF),
            pltpu.VMEM((pairs, seq, LANES), BF),
            pltpu.VMEM((seq, LANES), BF),
            pltpu.VMEM((seq, LANES), F32),
            pltpu.VMEM((seq, 3 * width), BF),
            pltpu.VMEM((width, seq), BF),
        ],
        compiler_params=params(60),
        cost_estimate=pl.CostEstimate(flops=60 * 10**9, bytes_accessed=24 * 10**6, transcendentals=0),
        name="attention_backward",
    )(lengths, x, g, normed, qkv, mixed, laug, h, ing_ret, slot_col, w_qkv, w_out, g1, g2)

    output = pl.pallas_call(
        collect_kernel,
        out_shape=sds((seq, width), F32),
        in_specs=[VMEM] * 3,
        out_specs=VMEM,
        compiler_params=params(40),
        name="collect_output",
    )(h, slot_col, ffn_ret)

    in_sum = lax.psum(wing, "dp").astype(F32)
    back_sum = lax.psum(wbg, "dp").astype(F32)
    both = ("dp", "expert")
    out_sum = lax.psum(woutg, both).astype(F32)
    qkv_sum = lax.psum(wqkvg, both).astype(F32)
    g1_sum, g2_sum = lax.psum((g1g[0], g2g[0]), both)
    return (
        output[None], tokg[None], qkv_sum, out_sum, g1_sum, g2_sum, in_sum[None], back_sum[None],
    )


def exchange(rows, experts):
    total, width = rows.shape
    rows = rows.reshape(experts, total // experts, width)
    return lax.all_to_all(rows, "expert", split_axis=0, concat_axis=0, tiled=True).reshape(total, width)


def solution(mesh):
    split = P(("dp", "expert"), None, None)
    mine = P("expert", None, None)
    return jax.shard_map(
        functools.partial(shards, mesh.shape["expert"]),
        mesh=mesh,
        in_specs=(split, P(("dp", "expert")), split, P(), P(), P(), P(), mine, mine, split),
        out_specs=(split, split, P(), P(), P(), P(), mine, mine),
        check_vma=False,
    )
```

time: 846 us -> 548 us (0.65); the launches traced: 836 us -> 547 us
  matrix products: 280 us -> 0 us
  Pallas kernels: 0 us -> 158 us
  blocking collectives: 48.9 us -> 175 us
  local copies, waits for them, and re-layouts: 132 us -> 6.26 us
  other arithmetic: 123 us -> 18.5 us
  waiting for transfers between devices: 193 us -> 162 us
  starting transfers between devices: 41.9 us -> 12.5 us
    dot_general x26 -> x0, matrix products: 280 us -> none  [the longest x4 63.8 us: block_scores(): jnp.einsum('qhd,khd->hqk', query_block, key_heads, preferred_element_type...]
    pallas_call x0 -> x5, Pallas kernels: none -> 158 us  [the longest x1 54.7 us: shards(): pl.pallas_call(expert_kernel, grid=(ff // tile,), out_shape=(sds((total,...]
    all_to_all x0 -> x2, blocking collectives: none -> 123 us  [exchange(): lax.all_to_all(rows, 'expert', split_axis=0, concat_axis=0, tiled=True)]
    convert_element_type x6 -> x2, other arithmetic: 57.5 us -> 6.47 us  [the longest x1 3.48 us: shards(): qkv_sum = lax.psum(wqkvg, both).astype(F32)]
    reduce_sum x7 -> x0, other arithmetic: 35.2 us -> none  [the longest x2 25.4 us: forward_block(): row_total = jnp.sum(exponent, axis=-1, keepdims=True)]
    all_to_all x4 -> x2, starting transfers between devices: 41.2 us -> 12.4 us  [exchange(): lax.all_to_all(rows, 'expert', split_axis=0, concat_axis=0, tiled=True)]
    unnamed x75 -> x24, local copies, waits for them, and re-layouts: 31.9 us -> 4.07 us
    psum x2, waiting for transfers between devices: 119 us -> 95.2 us  [the longest x1 58.7 us: shards(): qkv_sum = lax.psum(wqkvg, both).astype(F32)]
  transfers between devices with their start and end apart: 6 -> 4, of which waited for: 5 -> 4; matrix products, arithmetic and copies ran while one was open for 45% -> 2% of each run, Pallas kernels for 0% -> 8%
where the time goes in v1:
time: 548 us; the launch traced here: 547 us
  blocking collectives  175 us (32%)
  waiting for transfers between devices  162 us (30%)
  Pallas kernels  158 us (29%)
  other arithmetic  18.5 us (3%)
  between operations  14.8 us (3%)
  starting transfers between devices  12.5 us (2%)
  local copies, waits for them, and re-layouts  6.26 us (1%)
    all_to_all x2, blocking collectives, exchange(): lax.all_to_all(rows, 'expert', split_axis=0, concat_axis=0, tiled=True)  123 us
    all_to_all x2, waiting for transfers between devices, exchange(): lax.all_to_all(rows, 'expert', split_axis=0, concat_axis=0, tiled=True)  66.1 us
    psum x1, waiting for transfers between devices, shards(): qkv_sum = lax.psum(wqkvg, both).astype(F32)  58.7 us
    pallas_call x1, Pallas kernels, shards(): pl.pallas_call(expert_kernel, grid=(ff // tile,), out_shape=(sds((total,...  54.7 us
    pallas_call x1, Pallas kernels, shards(): pl.pallas_call(backward_kernel, out_shape=(sds((seq, width), F32), sds((w...  52.2 us
    psum x1, blocking collectives, shards(): g1_sum, g2_sum = lax.psum((g1g[0], g2g[0]), both)  52 us
    pallas_call x1, Pallas kernels, shards(): pl.pallas_call(functools.partial(forward_kernel, experts, capacity), out_...  41.1 us
    psum x1, waiting for transfers between devices, shards(): in_sum = lax.psum(wing, 'dp').astype(F32)  36.5 us
  transfers between devices with their start and end apart: 4, of which 4 were waited for; matrix products, arithmetic and copies ran while one was open for 2% of the time, Pallas kernels for 8%

profile of v1, /device:TPU:0, one launch (start us, length us, event | category | flops | bytes accessed | tf_op | source)
XLA Modules:
  0.0 547.5 jit_solution(11803941850728447051)
XLA Ops:
  7.8 0.0 copy-start.1
  7.8 1.4 copy-done.1
  9.2 0.7 copy-done.3
  9.9 4.9 place_gradient.1
  14.8 8.5 %all-to-all-start.1 = ((bf16[16,96,768]{2,1,0:T(8,128)(2,1)}), bf16[16,96,768]{2,1,0:T(8,128)(2,1)S(1)}, u32[]{:S(2)}, u32[]{:S(2)}) async-start(bf16[16,96,768]{2,1,0:T(8,128)(2,1)} %bitcast.6), calls=%async_computation.1 | async-start | bytes 4718592 | tf_op jit(solution)/shard_map/all_to_all | solution.py:463
  23.3 0.0 all-reduce.6.cloned.1.call-start
  23.3 0.0 copy-done.8
  23.3 0.6 reshape.50.g1_ref
  23.9 0.6 reshape.51.g2_ref
  24.5 1.0 copy.18.eid_col_ref
  25.5 41.1 %attention_forward.1 = (bf16[1024,768]{1,0:T(8,128)(2,1)}, bf16[18,1024,128]{2,1,0:T(8,128)(2,1)}, bf16[1024,768]{1,0:T(8,128)(2,1)}, bf16[6,1024,128]{2,1,0:T(8...) custom-call(s32[1]{0:T(128)S(6)} %copy.23.len_ref, bf16[1024,768]{1,0:T(8,128)(2,1)} %bitcast.35, ...), custom_call_target="tpu_custom_call" | custom-call | flops 40000000000 | bytes 24000000 | tf_op jit(solution)/shard_map/attention_forward/pallas_call | solution.py:359
  66.6 4.3 all-to-all-done.1
  70.9 65.5 %all_to_all.20 = bf16[16,96,768]{2,1,0:T(8,128)(2,1)} all-to-all(bf16[16,96,768]{2,1,0:T(8,128)(2,1)} %bitcast.30), channel_id=1, replica_groups=mesh['dp'=2,'expert'=16] {'expert'}, dimensions={0} | all-to-all | bytes 4718592 | tf_op jit(solution)/shard_map/all_to_all | solution.py:463
  136.3 54.7 %experts.1 = (bf16[1536,768]{1,0:T(8,128)(2,1)}, bf16[1536,768]{1,0:T(8,128)(2,1)}, bf16[768,3072]{1,0:T(8,128)(2,1)}, bf16[3072,768]{1,0:T(8,128)(2,1)}) custom-call(bf16[1536,768]{1,0:T(8,128)(2,1)} %bitcast.31, bf16[1536,768]{1,0:T(8,128)(2,1)} %bitcast.28, bf16[768,3072]{1,0:T(8,128)(2,1)} %bitcast.33, bf16[3072,768]{1,0:T(8,128)(2,1)} %bitcast.34), custom_call_target="tpu_custom_call" | custom-call | flops 44000002048 | bytes 30000000 | tf_op jit(solution)/shard_map/experts/pallas_call | solution.py:385
  191.0 58.0 %all_to_all.21 = bf16[16,96,768]{2,1,0:T(8,128)(2,1)} all-to-all(bf16[16,96,768]{2,1,0:T(8,128)(2,1)} %bitcast.32), channel_id=1, replica_groups=mesh['dp'=2,'expert'=16] {'expert'}, dimensions={0} | all-to-all | bytes 4718592 | tf_op jit(solution)/shard_map/all_to_all | solution.py:463
  249.0 52.2 %attention_backward.1 = (f32[1024,768]{1,0:T(8,128)}, bf16[768,2304]{1,0:T(8,128)(2,1)}, bf16[768,768]{1,0:T(8,128)(2,1)}, f32[1,768]{1,0:T(1,128)}, f32[1,768]{1,0:T(1,128)}) custom-call(s32[1]{0:T(128)S(6)} %copy.23.len_ref, bf16[1024,768]{1,0:T(8,128)(2,1)} %bitcast.36, bf16[1024,768]{1,0:T(8,128)(2,1)} %bitcast.19, ...), custom_call_target="tpu_custom_call" | custom-call | flops 60000002048 | bytes 24000000 | tf_op jit(solution)/shard_map/attention_backward/pallas_call | solution.py:414
  301.2 0.0 all-reduce.6.cloned.1.call-update
  301.2 0.0 all-reduce.8.cloned.1.call-start
  301.2 0.7 all-reduce.8.cloned.1.call-update
  302.0 3.9 all-to-all-start.2
  305.9 0.0 copy-done.11
  305.9 0.0 copy-done.10
  306.0 61.8 %all-to-all-done.2 = bf16[16,96,768]{2,1,0:T(8,128)(2,1)S(1)} async-done(((bf16[16,96,768]{2,1,0:T(8,128)(2,1)}), bf16[16,96,768]{2,1,0:T(8,128)(2,1)S(1)}, u32[]{:S(2)}, u32[]{:S(2)}) %all-to-all-start.2) | async-done | bytes 2359328 | tf_op jit(solution)/shard_map/all_to_all | solution.py:463
  367.8 1.9 copy-done
  369.7 5.2 collect_output.1
  375.0 52.0 %all-reduce = (f32[768]{0:T(1024)}, f32[768]{0:T(1024)}) all-reduce(f32[768]{0:T(1024)S(1)} %reduce, f32[768]{0:T(1024)S(1)} %reduce.1), channel_id=1, replica_groups=mesh['dp'=2,'expert'=16] {'dp','expert'}, use_global_device_ids=true, to_apply=%region_2.0 | all-reduce | flops 1536 | bytes 12288 | tf_op jit(solution)/shard_map/psum | solution.py:454
  427.0 58.7 %all-reduce.6.cloned.1.call-done = (bf16[768,2304]{1,0:T(8,128)(2,1)}, bf16[768,768]{1,0:T(8,128)(2,1)}) async-done(((bf16[768,2304]{1,0:T(8,128)(2,1)}, bf16[768,768]{1,0:T(8,128)(2,1)}), (bf16[768,2304]{1,0:T(8,128)(2,1)}, bf16[768,768]{1,0:T(8,128)(2,1)})) %all-reduce.6.cloned.1.call-update) | async-done | bytes 4718608 | tf_op jit(solution)/shard_map/psum | solution.py:453
  485.7 3.0 convert_element_type.9
  488.7 3.5 convert_element_type.8
  492.2 36.5 %all-reduce.8.cloned.1.call-done = (bf16[1,768,3072]{2,1,0:T(8,128)(2,1)}, bf16[1,3072,768]{2,1,0:T(8,128)(2,1)}) async-done(((bf16[1,768,3072]{2,1,0:T(8,128)(2,1)}, bf16[1,3072,768]{2,1,0:T(8,128)(2,1)}), (bf16[1,768,3072]{2,1,0:T(8,128)(2,1)}, bf16[1,3072,768]{2,1,0:T(8,128)(2,1)})) %all-reduce.8.cloned.1.call-update) | async-done | bytes 9437200 | tf_op jit(solution)/shard_map/psum | solution.py:449
  528.7 7.5 %broadcast_in_dim.21 = f32[1,768,3072]{2,1,0:T(8,128)} convert(bf16[1,768,3072]{2,1,0:T(8,128)(2,1)} %get-tuple-element.46) | non-fusion elementwise | flops 2359296 | bytes 14155776 | tf_op jit(solution)/shard_map/broadcast_in_dim | solution.py:456
  536.2 4.5 broadcast_in_dim.23
  (19 shorter events, 0.1 us)
Async XLA Ops:
  7.8 1.4 copy-start.1
  9.2 0.7 copy-start.3
  14.8 8.5 %copy-start.8 = (f32[768]{0:T(1024)S(1)}, f32[768]{0:T(1024)}, u32[]{:S(2)}) copy-start(f32[768]{0:T(1024)} %param.15) | copy-start | bytes 9220
  14.8 9.1 %copy-start.9 = (f32[768]{0:T(1024)S(1)}, f32[768]{0:T(1024)}, u32[]{:S(2)}) copy-start(f32[768]{0:T(1024)} %param.16) | copy-start | bytes 9220
  14.8 9.7 %copy-start.4 = (s32[1,1024,1]{1,2,0:T(1,128)S(1)}, s32[1,1024,1]{1,2,0:T(1,128)}, u32[]{:S(2)}) copy-start(s32[1,1024,1]{1,2,0:T(1,128)} %param.12) | copy-start | bytes 12292
  14.8 56.1 %all-to-all-start.1 = ((bf16[16,96,768]{2,1,0:T(8,128)(2,1)}), bf16[16,96,768]{2,1,0:T(8,128)(2,1)S(1)}, u32[]{:S(2)}, u32[]{:S(2)}) async-start(bf16[16,96,768]{2,1,0:T(8,128)(2,1)} %bitcast.6), calls=%async_computation.1 | async-start | bytes 4718592 | tf_op jit(solution)/shard_map/all_to_all | solution.py:463
  23.3 462.4 %all-reduce.6.cloned.1.call-start = ((), (), s32[]{:S(2)}) async-start(), calls=%async_computation.4 | async-start | bytes 9437184 | tf_op jit(solution)/shard_map/psum | solution.py:453
  70.9 65.5 %copy-start.7 = (bf16[16,96,768]{2,1,0:T(8,128)(2,1)}, bf16[16,96,768]{2,1,0:T(8,128)(2,1)S(1)}, u32[]{:S(2)}) copy-start(bf16[16,96,768]{2,1,0:T(8,128)(2,1)S(1)} %all-to-all-done.1) | copy-start | bytes 7077892
  301.2 227.5 %all-reduce.8.cloned.1.call-start = ((), (), s32[]{:S(2)}) async-start(), calls=%async_computation.5 | async-start | bytes 18874368 | tf_op jit(solution)/shard_map/psum | solution.py:449
  301.9 4.0 copy-start.11
  301.9 4.0 copy-start.10
  302.0 65.8 %copy-start.2 = (s32[1024,1]{1,0:T(8,128)S(1)}, s32[1024,1]{1,0:T(8,128)}, u32[]{:S(2)}) copy-start(s32[1024,1]{1,0:T(8,128)} %get-tuple-element.26.slot_col_ref) | copy-start | bytes 12292
  302.0 65.8 %all-to-all-start.2 = ((bf16[16,96,768]{2,1,0:T(8,128)(2,1)}), bf16[16,96,768]{2,1,0:T(8,128)(2,1)S(1)}, u32[]{:S(2)}, u32[]{:S(2)}) async-start(bf16[16,96,768]{2,1,0:T(8,128)(2,1)} %bitcast.27), calls=%async_computation.2 | async-start | bytes 4718592 | tf_op jit(solution)/shard_map/all_to_all | solution.py:463
  367.8 1.9 copy-start
  485.7 3.0 copy-start.6
  528.7 7.5 %copy-start.5 = (bf16[1,3072,768]{2,1,0:T(8,128)(2,1)S(1)}, bf16[1,3072,768]{2,1,0:T(8,128)(2,1)}, u32[]{:S(2)}) copy-start(bf16[1,3072,768]{2,1,0:T(8,128)(2,1)} %get-tuple-element.47) | copy-start | bytes 14155780
Sparse Core Ops, SparseCore 0:
  301.3 184.3 all-reduce.5
  489.0 39.6 all-reduce.7

commit v2 on v1

--- a/solution.py
+++ b/solution.py
@@ -14,6 +14,8 @@
 EPS = 1e-5
 NEG = -1e30
 VMEM = pl.BlockSpec(memory_space=pltpu.VMEM)
+ANY = pl.BlockSpec(memory_space=pl.ANY)
+MESH = pl.DeviceIdType.MESH
 SMEM = pl.BlockSpec(memory_space=pltpu.SMEM)
 MIB = 2**20
 
@@ -209,37 +211,232 @@
         out_ref[r, :] = h_ref[r, :] + collect(slot_col_ref, ret_ref, r)
 
 
-def expert_kernel(x_ref, g_ref, win_ref, wback_ref, ffn_ref, ing_ref, wing_ref, wbg_ref, ffn_acc, ing_acc):
-    t = pl.program_id(0)
-    total = x_ref.shape[0]
-    tile = win_ref.shape[1]
-    blocks = 4
-    size = total // blocks
-
-    @pl.when(t == 0)
-    def _():
-        ffn_acc[...] = jnp.zeros_like(ffn_acc)
-        ing_acc[...] = jnp.zeros_like(ing_acc)
-
-    hidden_parts, act_parts = [], []
-    for i in range(blocks):
-        r = slice(i * size, (i + 1) * size)
-        a = dot(x_ref[r, :], win_ref[...])
-        gate = jax.nn.sigmoid(a)
-        hidden = (a * gate).astype(BF)
-        back = dot_t(g_ref[r, :], wback_ref[...])
-        act = (back * gate * (1.0 + a * (1.0 - gate))).astype(BF)
-        ffn_acc[r, :] += dot(hidden, wback_ref[...])
-        ing_acc[r, :] += dot_t(act, win_ref[...])
-        hidden_parts.append(hidden)
-        act_parts.append(act)
-    wing_ref[...] = tdot(x_ref[...], jnp.concatenate(act_parts, axis=0)).astype(BF)
-    wbg_ref[...] = tdot(jnp.concatenate(hidden_parts, axis=0), g_ref[...]).astype(BF)
-
-    @pl.when(t == pl.num_programs(0) - 1)
-    def _():
-        ffn_ref[...] = ffn_acc[...].astype(BF)
-        ing_ref[...] = ing_acc[...].astype(BF)
+def flip(v, j, size):
+    out, bit = 0, 1
+    while bit < size:
+        out = out + bit * ((v // bit + j // bit) % 2)
+        bit *= 2
+    return out
+
+
+def greet(experts, with_partner):
+    me = lax.axis_index("expert")
+    barrier = pltpu.get_barrier_semaphore()
+
+    @pl.loop(1, experts)
+    def _(j):
+        pl.semaphore_signal(
+            barrier, inc=1, device_id={"expert": flip(me, j, experts)}, device_id_type=MESH
+        )
+
+    if with_partner:
+        pl.semaphore_signal(
+            barrier, inc=1, device_id={"dp": 1 - lax.axis_index("dp")}, device_id_type=MESH
+        )
+    pl.semaphore_wait(barrier, experts - 1 + int(with_partner))
+
+
+def expert_kernel(
+    experts, capacity,
+    x_ref, g_ref, win_hbm, wback_hbm,
+    ing_ref, ffn_ref, wing_ref, wbg_ref,
+    xin, gin, win, wback, hidden, act, ing_out, xt, own_in, own_back, got_in, got_back,
+    x_send, x_recv, r_send, r_recv, g_sem, w_sem, own_sem, ffn_sem, t_send, t_recv, o_sem,
+):
+    me = lax.axis_index("expert")
+    other = 1 - lax.axis_index("dp")
+    width, ff = win.shape
+    groups, chunk = experts // 4, 4 * capacity
+
+    def block(j):
+        return pl.ds(pl.multiple_of(j * capacity, 16), capacity)
+
+    def x_copy(j):
+        peer = flip(me, j, experts)
+        return pltpu.make_async_remote_copy(
+            src_ref=x_ref.at[block(peer)], dst_ref=xin.at[block(j)],
+            send_sem=x_send.at[j], recv_sem=x_recv.at[j],
+            device_id={"expert": peer}, device_id_type=MESH,
+        )
+
+    def r_copy(j):
+        return pltpu.make_async_remote_copy(
+            src_ref=ing_out.at[block(j)], dst_ref=ing_ref.at[block(me)],
+            send_sem=r_send.at[j], recv_sem=r_recv.at[j],
+            device_id={"expert": flip(me, j, experts)}, device_id_type=MESH,
+        )
+
+    def g_copy(j):
+        return pltpu.make_async_copy(g_ref.at[block(flip(me, j, experts))], gin.at[block(j)], g_sem.at[j])
+
+    own_x = pltpu.make_async_copy(x_ref.at[block(me)], xin.at[block(0)], own_sem.at[0])
+    own_ing = pltpu.make_async_copy(ing_out.at[block(0)], ing_ref.at[block(me)], own_sem.at[1])
+    load_in = pltpu.make_async_copy(win_hbm, win, w_sem.at[0])
+    load_back = pltpu.make_async_copy(wback_hbm, wback, w_sem.at[1])
+    own_x.start()
+    load_in.start()
+    load_back.start()
+
+    @pl.loop(0, experts)
+    def _(j):
+        g_copy(j).start()
+
+    greet(experts, True)
+    for low, high in ((2, 3), (0, 2), (3, 4)):
+
+        @pl.loop(max(1, experts * low // 4), experts * high // 4)
+        def _(j):
+            x_copy(j).start()
+
+    own_x.wait()
+    load_in.wait()
+    load_back.wait()
+
+    @pl.loop(0, experts)
+    def _(j):
+        g_copy(j).wait()
+
+    def ffn_copy(j):
+        peer = flip(me, j, experts)
+        return pltpu.make_async_copy(xin.at[block(j)], ffn_ref.at[block(peer)], ffn_sem.at[j])
+
+    @pl.loop(0, groups)
+    def _(i):
+        r = rows_of(i, chunk)
+        for c in range(4):
+            j = 4 * i + c
+
+            @pl.when(j > 0)
+            def _():
+                x_copy(j).wait_recv()
+
+        @pl.loop(0, ff // 512)
+        def _(t):
+            c = rows_of(t, 512)
+            a = dot(xin[r, :], win[:, c])
+            gate = jax.nn.sigmoid(a)
+            hidden[r, c] = (a * gate).astype(BF)
+            back = dot_t(gin[r, :], wback[c, :])
+            act[r, c] = (back * gate * (1.0 + a * (1.0 - gate))).astype(BF)
+
+        @pl.loop(0, width // 256)
+        def _(n):
+            c = rows_of(n, 256)
+            ing_out[r, c] = dot_t(act[r, :], win[c, :]).astype(BF)
+
+        for c in range(4):
+            j = 4 * i + c
+
+            @pl.when(j > 0)
+            def _():
+                r_copy(j).start()
+
+        @pl.when(i == 0)
+        def _():
+            own_ing.start()
+
+        xt[:, r] = xin[r, :].T
+
+        @pl.loop(0, width // 256)
+        def _(n):
+            c = rows_of(n, 256)
+            xin[r, c] = dot(hidden[r, :], wback[:, c]).astype(BF)
+
+        for c in range(4):
+            ffn_copy(4 * i + c).start()
+
+    tiles = ff // 256
+
+    def sends(t):
+        s = t % 4
+        to = dict(device_id={"dp": other}, device_id_type=MESH)
+        return (
+            pltpu.make_async_remote_copy(own_in.at[s], got_in.at[t], t_send.at[0, t], t_recv.at[0, t], **to),
+            pltpu.make_async_remote_copy(own_back.at[s], got_back.at[t], t_send.at[1, t], t_recv.at[1, t], **to),
+        )
+
+    def writes(t):
+        s, c = t % 4, rows_of(t, 256)
+        return (
+            pltpu.make_async_copy(own_in.at[s], wing_ref.at[:, c], o_sem.at[0, s]),
+            pltpu.make_async_copy(own_back.at[s], wbg_ref.at[c, :], o_sem.at[1, s]),
+        )
+
+    @pl.loop(0, tiles + 2)
+    def _(t):
+        @pl.when(t < tiles)
+        def _():
+            s, c = t % 4, rows_of(t, 256)
+
+            @pl.when(t >= 4)
+            def _():
+                for copy in writes(t - 4):
+                    copy.wait()
+
+            own_in[s] = dot(xt[...], act[:, c]).astype(BF)
+            own_back[s] = tdot(hidden[:, c], gin[...]).astype(BF)
+            for copy in sends(t):
+                copy.start()
+
+        @pl.when(t >= 2)
+        def _():
+            u = t - 2
+            for copy in sends(u):
+                copy.wait()
+            s = u % 4
+            own_in[s] = (own_in[s].astype(F32) + got_in[u].astype(F32)).astype(BF)
+            own_back[s] = (own_back[s].astype(F32) + got_back[u].astype(F32)).astype(BF)
+            for copy in writes(u):
+                copy.start()
+
+    for u in range(tiles - 4, tiles):
+        for copy in writes(u):
+            copy.wait()
+    own_ing.wait()
+
+    @pl.loop(0, experts)
+    def _(j):
+        ffn_copy(j).wait()
+
+    @pl.loop(1, experts)
+    def _(j):
+        x_copy(j).wait_send()
+        r_copy(j).wait()
+
+
+def experts_call(experts, capacity, x_slots, g_slots, w_in, w_back):
+    total, width = x_slots.shape
+    ff = w_in.shape[1]
+    tiles = ff // 256
+    dma = pltpu.SemaphoreType.DMA
+    return pl.pallas_call(
+        functools.partial(expert_kernel, experts, capacity),
+        out_shape=(
+            sds((total, width), BF), sds((total, width), BF), sds((width, ff), BF), sds((ff, width), BF),
+        ),
+        in_specs=[ANY] * 4,
+        out_specs=(ANY,) * 4,
+        scratch_shapes=[
+            pltpu.VMEM((total, width), BF),
+            pltpu.VMEM((total, width), BF),
+            pltpu.VMEM((width, ff), BF),
+            pltpu.VMEM((ff, width), BF),
+            pltpu.VMEM((total, ff), BF),
+            pltpu.VMEM((total, ff), BF),
+            pltpu.VMEM((total, width), BF),
+            pltpu.VMEM((width, total), BF),
+            pltpu.VMEM((4, width, 256), BF),
+            pltpu.VMEM((4, 256, width), BF),
+            pltpu.VMEM((tiles, width, 256), BF),
+            pltpu.VMEM((tiles, 256, width), BF),
+            dma((experts,)), dma((experts,)), dma((experts,)), dma((experts,)),
+            dma((experts,)), dma((2,)), dma((2,)), dma((experts,)),
+            dma((2, tiles)), dma((2, tiles)), dma((2, 4)),
+        ],
+        compiler_params=params(61, collective_id=1, has_side_effects=True),
+        cost_estimate=pl.CostEstimate(flops=44 * 10**9, bytes_accessed=30 * 10**6, transcendentals=0),
+        name="experts",
+    )(x_slots, g_slots, w_in, w_back)
 
 
 def backward_kernel(
@@ -344,7 +541,6 @@
     eid_row = expert_ids.reshape(1, seq)
     eid_col = expert_ids[0]
     g1, g2 = norm1_gain.reshape(1, width), norm2_gain.reshape(1, width)
-    ff = w_in.shape[2]
 
     g_slots, _ = pl.pallas_call(
         functools.partial(place_kernel, experts, capacity),
@@ -378,37 +574,7 @@
         cost_estimate=pl.CostEstimate(flops=40 * 10**9, bytes_accessed=24 * 10**6, transcendentals=0),
         name="attention_forward",
     )(lengths, x, eid_row, eid_col, w_qkv, w_out, g1, g2)
-    x_in = exchange(x_slots, experts)
-
-    tile = 512
-    full = pl.BlockSpec((total, width), lambda t: (0, 0))
-    ffn, ing, wing, wbg = pl.pallas_call(
-        expert_kernel,
-        grid=(ff // tile,),
-        out_shape=(
-            sds((total, width), BF),
-            sds((total, width), BF),
-            sds((width, ff), BF),
-            sds((ff, width), BF),
-        ),
-        in_specs=[
-            full,
-            full,
-            pl.BlockSpec((width, tile), lambda t: (0, t)),
-            pl.BlockSpec((tile, width), lambda t: (t, 0)),
-        ],
-        out_specs=(
-            full,
-            full,
-            pl.BlockSpec((width, tile), lambda t: (0, t)),
-            pl.BlockSpec((tile, width), lambda t: (t, 0)),
-        ),
-        scratch_shapes=[pltpu.VMEM((total, width), F32)] * 2,
-        compiler_params=params(58),
-        cost_estimate=pl.CostEstimate(flops=44 * 10**9, bytes_accessed=30 * 10**6, transcendentals=0),
-        name="experts",
-    )(x_in, g_in, w_in[0], w_back[0])
-    ing_ret = exchange(ing, experts)
+    ing_ret, ffn, wing, wbg = experts_call(experts, capacity, x_slots, g_in, w_in[0], w_back[0])
     ffn_ret = exchange(ffn, experts)
 
     tokg, wqkvg, woutg, g1g, g2g = pl.pallas_call(
@@ -446,8 +612,8 @@
         name="collect_output",
     )(h, slot_col, ffn_ret)
 
-    in_sum = lax.psum(wing, "dp").astype(F32)
-    back_sum = lax.psum(wbg, "dp").astype(F32)
+    in_sum = wing.astype(F32)
+    back_sum = wbg.astype(F32)
     both = ("dp", "expert")
     out_sum = lax.psum(woutg, both).astype(F32)
     qkv_sum = lax.psum(wqkvg, both).astype(F32)

time: 548 us -> 421 us (0.77)
  blocking collectives: 175 us -> 41.2 us
  waiting for transfers between devices: 162 us -> 94.9 us
  Pallas kernels: 158 us -> 208 us
  starting transfers between devices: 12.5 us -> 33.3 us
    all_to_all x2 -> x0, blocking collectives: 123 us -> none  [exchange(): lax.all_to_all(rows, 'expert', split_axis=0, concat_axis=0, tiled=True)]
    all_to_all x2, waiting for transfers between devices: 66.1 us -> 4.35 us  [exchange(): lax.all_to_all(rows, 'expert', split_axis=0, concat_axis=0, tiled=True)]
    pallas_call x1, Pallas kernels: 54.7 us -> 104 us  [experts_call(): pl.pallas_call(functools.partial(expert_kernel, experts, capacity), out_s...]
    psum x1 -> x0, waiting for transfers between devices: 36.5 us -> none  [shards(): in_sum = lax.psum(wing, 'dp').astype(F32)]
    psum x1, waiting for transfers between devices: 58.7 us -> 90.5 us  [shards(): qkv_sum = lax.psum(wqkvg, both).astype(F32)]
    all_to_all x2, starting transfers between devices: 12.4 us -> 33.1 us  [exchange(): lax.all_to_all(rows, 'expert', split_axis=0, concat_axis=0, tiled=True)]
    psum x1, blocking collectives: 52 us -> 41.2 us  [shards(): g1_sum, g2_sum = lax.psum((g1g[0], g2g[0]), both)]
  transfers between devices with their start and end apart: 4 -> 3, of which waited for: 4 -> 2; matrix products, arithmetic and copies ran while one was open for 2% -> 5% of each run, Pallas kernels for 8% -> 22%
where the time goes in v2:
time: 421 us
  Pallas kernels  208 us (49%)
  waiting for transfers between devices  94.9 us (23%)
  blocking collectives  41.2 us (10%)
  starting transfers between devices  33.3 us (8%)
  other arithmetic  20.8 us (5%)
  between operations  14.8 us (4%)
  local copies, waits for them, and re-layouts  8.23 us (2%)
    pallas_call x1, Pallas kernels, experts_call(): pl.pallas_call(functools.partial(expert_kernel, experts, capacity), out_s...  104 us
    psum x1, waiting for transfers between devices, shards(): qkv_sum = lax.psum(wqkvg, both).astype(F32)  90.5 us
    pallas_call x1, Pallas kernels, shards(): pl.pallas_call(backward_kernel, out_shape=(sds((seq, width), F32), sds((w...  52.2 us
    psum x1, blocking collectives, shards(): g1_sum, g2_sum = lax.psum((g1g[0], g2g[0]), both)  41.2 us
    pallas_call x1, Pallas kernels, shards(): pl.pallas_call(functools.partial(forward_kernel, experts, capacity), out_...  41.1 us
    all_to_all x2, starting transfers between devices, exchange(): lax.all_to_all(rows, 'expert', split_axis=0, concat_axis=0, tiled=True)  33.1 us
  transfers between devices with their start and end apart: 3, of which 2 were waited for; matrix products, arithmetic and copies ran while one was open for 5% of the time, Pallas kernels for 22%

profile of v2, /device:TPU:0, one launch (start us, length us, event | category | flops | bytes accessed | tf_op | source)
XLA Modules:
  0.0 420.7 jit_solution(9344337692636638252)
XLA Ops:
  7.8 0.0 copy-start.1
  7.8 1.4 copy-done.1
  9.2 0.7 copy-done.3
  9.9 4.9 %place_gradient.1 = (bf16[1536,768]{1,0:T(8,128)(2,1)}, s32[1,1024]{1,0:T(1,128)}) custom-call(s32[1]{0:T(128)S(6)} %copy.21.len_ref, s32[1,1024]{1,0:T(1,128)S(1)} %bitcast.22, bf16[1024,768]{1,0:T(8,128)(2,1)S(1)} %bitcast.20), custom_call_target="tpu_custom_call" | custom-call | tf_op jit(solution)/shard_map/place_gradient/pallas_call | solution.py:545
  14.8 8.3 %all-to-all-start = ((bf16[16,96,768]{2,1,0:T(8,128)(2,1)}), bf16[16,96,768]{2,1,0:T(8,128)(2,1)S(1)}, u32[]{:S(2)}, u32[]{:S(2)}) async-start(bf16[16,96,768]{2,1,0:T(8,128)(2,1)} %bitcast.4), calls=%async_computation | async-start | bytes 4718592 | tf_op jit(solution)/shard_map/all_to_all | solution.py:629
  23.1 0.0 copy-done.7
  23.1 0.6 reshape.38.g1_ref
  23.7 0.0 copy-done.8
  23.7 0.6 reshape.39.g2_ref
  24.3 0.0 copy-done.4
  24.3 1.0 copy.18.eid_col_ref
  25.3 41.1 %attention_forward.1 = (bf16[1024,768]{1,0:T(8,128)(2,1)}, bf16[18,1024,128]{2,1,0:T(8,128)(2,1)}, bf16[1024,768]{1,0:T(8,128)(2,1)}, bf16[6,1024,128]{2,1,0:T(8...) custom-call(s32[1]{0:T(128)S(6)} %copy.21.len_ref, bf16[1024,768]{1,0:T(8,128)(2,1)} %bitcast.29, ...), custom_call_target="tpu_custom_call" | custom-call | flops 40000000000 | bytes 24000000 | tf_op jit(solution)/shard_map/attention_forward/pallas_call | solution.py:555
  66.4 4.3 %all-to-all-done = bf16[16,96,768]{2,1,0:T(8,128)(2,1)S(1)} async-done(((bf16[16,96,768]{2,1,0:T(8,128)(2,1)}), bf16[16,96,768]{2,1,0:T(8,128)(2,1)S(1)}, u32[]{:S(2)}, u32[]{:S(2)}) %all-to-all-start) | async-done | bytes 2359328 | tf_op jit(solution)/shard_map/all_to_all | solution.py:629
  70.7 1.4 copy-done.6
  72.1 104.2 %experts.1 = (bf16[1536,768]{1,0:T(8,128)(2,1)}, bf16[1536,768]{1,0:T(8,128)(2,1)}, bf16[768,3072]{1,0:T(8,128)(2,1)}, bf16[3072,768]{1,0:T(8,128)(2,1)}) custom-call(bf16[1536,768]{1,0:T(8,128)(2,1)} %get-tuple-element.27.x_ref, bf16[1536,768]{1,0:T(8,128)(2,1)} %bitcast.26, bf16[768,3072]{1,0:T(8,128)(2,1)} %bitcast.27, bf16[3072,768]{1,0:T(8,128)(2,1)} %bitcast.28), custom_call_target="tpu_custom_call" | custom-call | flops 44000002048 | bytes 30000000 | tf_op jit(solution)/shard_map/experts/pallas_call | solution.py:412
  176.4 24.8 %all-to-all-start.1 = ((bf16[16,96,768]{2,1,0:T(8,128)(2,1)}), bf16[16,96,768]{2,1,0:T(8,128)(2,1)S(1)}, u32[]{:S(2)}, u32[]{:S(2)}) async-start(bf16[16,96,768]{2,1,0:T(8,128)(2,1)} %bitcast.25), calls=%async_computation.1 | async-start | bytes 4718592 | tf_op jit(solution)/shard_map/all_to_all | solution.py:629
  201.2 0.2 all-reduce.4.cloned.1.call-start
  201.4 52.2 %attention_backward.1 = (f32[1024,768]{1,0:T(8,128)}, bf16[768,2304]{1,0:T(8,128)(2,1)}, bf16[768,768]{1,0:T(8,128)(2,1)}, f32[1,768]{1,0:T(1,128)}, f32[1,768]{1,0:T(1,128)}) custom-call(s32[1]{0:T(128)S(6)} %copy.21.len_ref, bf16[1024,768]{1,0:T(8,128)(2,1)} %bitcast.30, bf16[1024,768]{1,0:T(8,128)(2,1)} %bitcast.19, ...), custom_call_target="tpu_custom_call" | custom-call | flops 60000002048 | bytes 24000000 | tf_op jit(solution)/shard_map/attention_backward/pallas_call | solution.py:580
  253.6 0.0 copy-start.9
  253.6 0.0 all-reduce.4.cloned.1.call-update
  253.6 0.6 copy-done.10
  254.2 0.0 copy-done.9
  254.3 41.2 %all-reduce = (f32[768]{0:T(1024)}, f32[768]{0:T(1024)}) all-reduce(f32[768]{0:T(1024)S(1)} %reduce, f32[768]{0:T(1024)S(1)} %reduce.1), channel_id=1, replica_groups=mesh['dp'=2,'expert'=16] {'dp','expert'}, use_global_device_ids=true, to_apply=%region_2.0 | all-reduce | flops 1536 | bytes 12288 | tf_op jit(solution)/shard_map/psum | solution.py:620
  295.4 7.4 %bitcast_convert_fusion.1 = f32[1,768,3072]{2,1,0:T(8,128)} fusion(bf16[768,3072]{1,0:T(8,128)(2,1)} %get-tuple-element.40), kind=kLoop, calls=%fused_computation.1 | loop fusion | flops 2359296 | bytes 14155776 | tf_op jit(solution)/shard_map/broadcast_in_dim | solution.py:622
  302.8 6.9 %bitcast_convert_fusion = f32[1,3072,768]{2,1,0:T(8,128)} fusion(bf16[3072,768]{1,0:T(8,128)(2,1)} %get-tuple-element.41), kind=kLoop, calls=%fused_computation | loop fusion | flops 2359296 | bytes 14155776 | tf_op jit(solution)/shard_map/broadcast_in_dim | solution.py:622
  309.7 90.5 %all-reduce.4.cloned.1.call-done = (bf16[768,2304]{1,0:T(8,128)(2,1)}, bf16[768,768]{1,0:T(8,128)(2,1)}) async-done(((bf16[768,2304]{1,0:T(8,128)(2,1)}, bf16[768,768]{1,0:T(8,128)(2,1)}), (bf16[768,2304]{1,0:T(8,128)(2,1)}, bf16[768,768]{1,0:T(8,128)(2,1)})) %all-reduce.4.cloned.1.call-update) | async-done | bytes 4718608 | tf_op jit(solution)/shard_map/psum | solution.py:619
  400.2 3.0 convert_element_type.9
  403.2 0.0 copy-done.5
  403.2 3.5 convert_element_type.8
  406.7 0.0 all-to-all-done.1
  406.7 1.9 copy-done
  408.6 5.2 %collect_output.1 = f32[1024,768]{1,0:T(8,128)} custom-call(f32[1024,768]{1,0:T(8,128)S(1)} %copy-done, s32[1024,1]{1,0:T(8,128)S(1)} %copy-done.2, bf16[1536,768]{1,0:T(8,128)(2,1)S(1)} %bitcast.18), custom_call_target="tpu_custom_call" | custom-call | tf_op jit(solution)/shard_map/collect_output/pallas_call | solution.py:606
  (12 shorter events, 0.0 us)
Async XLA Ops:
  7.8 1.4 copy-start.1
  9.2 0.7 copy-start.3
  9.9 13.2 %copy-start.7 = (f32[768]{0:T(1024)S(1)}, f32[768]{0:T(1024)}, u32[]{:S(2)}) copy-start(f32[768]{0:T(1024)} %param.15) | copy-start | bytes 9220
  9.9 13.8 %copy-start.8 = (f32[768]{0:T(1024)S(1)}, f32[768]{0:T(1024)}, u32[]{:S(2)}) copy-start(f32[768]{0:T(1024)} %param.16) | copy-start | bytes 9220
  9.9 14.4 %copy-start.4 = (s32[1,1024,1]{1,2,0:T(1,128)S(1)}, s32[1,1024,1]{1,2,0:T(1,128)}, u32[]{:S(2)}) copy-start(s32[1,1024,1]{1,2,0:T(1,128)} %param.12) | copy-start | bytes 12292
  14.8 55.9 %all-to-all-start = ((bf16[16,96,768]{2,1,0:T(8,128)(2,1)}), bf16[16,96,768]{2,1,0:T(8,128)(2,1)S(1)}, u32[]{:S(2)}, u32[]{:S(2)}) async-start(bf16[16,96,768]{2,1,0:T(8,128)(2,1)} %bitcast.4), calls=%async_computation | async-start | bytes 4718592 | tf_op jit(solution)/shard_map/all_to_all | solution.py:629
  70.7 1.4 copy-start.6
  176.4 230.4 %all-to-all-start.1 = ((bf16[16,96,768]{2,1,0:T(8,128)(2,1)}), bf16[16,96,768]{2,1,0:T(8,128)(2,1)S(1)}, u32[]{:S(2)}, u32[]{:S(2)}) async-start(bf16[16,96,768]{2,1,0:T(8,128)(2,1)} %bitcast.25), calls=%async_computation.1 | async-start | bytes 4718592 | tf_op jit(solution)/shard_map/all_to_all | solution.py:629
  201.2 199.1 %all-reduce.4.cloned.1.call-start = ((), (), s32[]{:S(2)}) async-start(), calls=%async_computation.2 | async-start | bytes 9437184 | tf_op jit(solution)/shard_map/psum | solution.py:619
  253.6 0.7 copy-start.10
  253.6 0.7 copy-start.9
  400.2 3.0 copy-start.5
  403.2 3.5 copy-start.2
  406.7 1.9 copy-start
Sparse Core Ops, SparseCore 0:
  253.7 146.4 all-reduce.3

commit v3 on v2

--- a/solution.py
+++ b/solution.py
@@ -12,6 +12,7 @@
 LANES = 128
 ROWS = 256
 EPS = 1e-5
+LAGS = ((0, 1, 3, 4, 5, 7, 8), (0, 1, 3, 4, 5, 7, 8), (0, 1, 3, 4, 5, 6, 7), (0, 1, 2, 3, 4, 5, 6), (0, 1, 2, 3, 4, 5, 6))
 NEG = -1e30
 VMEM = pl.BlockSpec(memory_space=pltpu.VMEM)
 ANY = pl.BlockSpec(memory_space=pl.ANY)
@@ -84,13 +85,83 @@
 
 def forward_kernel(
     experts, capacity,
-    len_ref, tok_ref, eid_row_ref, eid_col_ref, wqkv_ref, wout_ref, g1_ref, g2_ref,
-    normed_ref, qkv_ref, mixed_ref, laug_ref, h_ref, slots_ref, slot_col_ref,
-    kaug_ref, xin_ref, slot_row_ref,
+    len_ref, eid_row_ref, eid_col_ref, g1_ref, g2_ref, tok_hbm, cot_hbm, wqkv_hbm, wout_hbm,
+    normed_out, qkv_out, mixed_out, laug_out, h_out, slots_out, slot_col_ref, g_got,
+    tok_ref, cot_ref, wqkv_ref, wout_ref, normed_ref, qkv_ref, mixed_ref, laug_ref, h_ref, slots_ref,
+    kaug_ref, xin_ref, slot_row_ref, gs_ref,
+    load_sem, store_sem, own_sem, g_send, g_recv,
 ):
     seq, width = tok_ref.shape
     blocks, pairs = seq // ROWS, width // LANES
+    total = experts * capacity
+    groups, chunk = experts // 4, 4 * capacity
     length = len_ref[0]
+    me = lax.axis_index("expert")
+
+    def block(j):
+        return pl.ds(pl.multiple_of(j * capacity, 16), capacity)
+
+    def g_copy(j):
+        peer = flip(me, j, experts)
+        return pltpu.make_async_remote_copy(
+            src_ref=gs_ref.at[block(peer)], dst_ref=g_got.at[block(j)],
+            send_sem=g_send.at[j], recv_sem=g_recv.at[j],
+            device_id={"expert": peer}, device_id_type=MESH,
+        )
+
+    own_g = pltpu.make_async_copy(gs_ref.at[block(me)], g_got.at[block(0)], own_sem)
+    loads = [
+        pltpu.make_async_copy(src, dst, load_sem.at[i])
+        for i, (src, dst) in enumerate(
+            ((cot_hbm, cot_ref), (tok_hbm, tok_ref), (wqkv_hbm, wqkv_ref), (wout_hbm, wout_ref))
+        )
+    ]
+    for copy in loads:
+        copy.start()
+    normed_copy, qkv_copy, mixed_copy, laug_copy, h_copy, slots_copy = [
+        pltpu.make_async_copy(src, dst, store_sem.at[i])
+        for i, (src, dst) in enumerate(
+            (
+                (normed_ref, normed_out), (qkv_ref, qkv_out), (mixed_ref, mixed_out), (laug_ref, laug_out),
+                (h_ref, h_out), (slots_ref, slots_out),
+            )
+        )
+    ]
+
+    tri = jnp.where(
+        lax.broadcasted_iota(I32, (seq, seq), 0) <= lane_iota((seq, seq)), 1.0, 0.0
+    ).astype(BF)
+    eid = eid_row_ref[...]
+    live = lane_iota((1, seq)) < length
+    pick = (lax.broadcasted_iota(I32, (experts, seq), 0) == eid) & live
+    pick = jnp.where(pick, 1.0, 0.0)
+    rank = jnp.sum(dot(pick.astype(BF), tri) * pick, axis=0, keepdims=True).astype(I32) - 1
+    slot_row_ref[...] = jnp.where(live, eid * capacity + rank, total)
+
+    greet(experts, False)
+    loads[0].wait()
+
+    def send_group(n):
+        place(slot_row_ref, cot_ref, gs_ref, flip(me // 4, n, groups), chunk)
+        for c in range(4):
+            j = 4 * n + c
+
+            @pl.when(j > 0)
+            def _():
+                g_copy(j).start()
+
+        @pl.when(n == 0)
+        def _():
+            own_g.start()
+
+    for low, high in ((groups // 2, groups), (0, groups // 2)):
+
+        @pl.loop(low, high)
+        def _(n):
+            send_group(n)
+
+    for copy in loads[1:]:
+        copy.wait()
 
     @pl.loop(0, blocks)
     def _(i):
@@ -106,6 +177,8 @@
             qkv_ref[2 * j, r, :] = out[:, :LANES]
             qkv_ref[2 * j + 1, r, :] = out[:, LANES:]
 
+    normed_copy.start()
+    qkv_copy.start()
     kaug_ref[...] = key_aug(seq, length)
     first = lane_iota((1, LANES)) < HEAD
     scale = jnp.asarray(HEAD**-0.5, BF)
@@ -138,6 +211,9 @@
             lse = jnp.where(first, tops[1], tops[0]) + jnp.log(below)
             laug_ref[p, r, :] = aug_of(lse, 1.0)
 
+    mixed_copy.start()
+    laug_copy.start()
+
     @pl.loop(0, blocks)
     def _(i):
         r = rows_of(i)
@@ -146,16 +222,13 @@
         hat, _ = normalize(h)
         xin_ref[r, :] = (hat * g2_ref[...]).astype(BF)
 
-    tri = jnp.where(
-        lax.broadcasted_iota(I32, (seq, seq), 0) <= lane_iota((seq, seq)), 1.0, 0.0
-    ).astype(BF)
-    eid = eid_row_ref[...]
-    live = lane_iota((1, seq)) < length
-    pick = (lax.broadcasted_iota(I32, (experts, seq), 0) == eid) & live
-    pick = jnp.where(pick, 1.0, 0.0)
-    rank = jnp.sum(dot(pick.astype(BF), tri) * pick, axis=0, keepdims=True).astype(I32) - 1
-    slot_row_ref[...] = jnp.where(live, eid * capacity + rank, experts * capacity)
-
+    h_copy.start()
+
+    @pl.loop(0, groups)
+    def _(n):
+        place(slot_row_ref, xin_ref, slots_ref, n, chunk)
+
+    slots_copy.start()
     eid = eid_col_ref[...]
     live = lax.broadcasted_iota(I32, (seq, 1), 0) < length
     pick = (lane_iota((seq, LANES)) == eid) & live
@@ -163,12 +236,13 @@
     rank = jnp.sum(tdot(tri, pick.astype(BF)) * pick, axis=1, keepdims=True).astype(I32) - 1
     slot_col_ref[...] = jnp.where(live, eid * capacity + rank, experts * capacity)
 
-    total = experts * capacity
-    step = 4 * capacity
-
-    @pl.loop(0, total // step)
-    def _(c):
-        place(slot_row_ref, xin_ref, slots_ref, c, step)
+    own_g.wait()
+    for copy in (normed_copy, qkv_copy, mixed_copy, laug_copy, h_copy, slots_copy):
+        copy.wait()
+
+    @pl.loop(1, experts)
+    def _(j):
+        g_copy(j).wait()
 
 
 def place(slot_row_ref, src_ref, slots_ref, c, step):
@@ -182,33 +256,6 @@
     total = ret_ref.shape[0]
     onehot = jnp.where(slot_col_ref[r, :] == lane_iota((ROWS, total)), 1.0, 0.0).astype(BF)
     return dot(onehot, ret_ref[...])
-
-
-def place_kernel(experts, capacity, len_ref, eid_row_ref, cot_ref, slots_ref, slot_row_ref):
-    seq, _ = cot_ref.shape
-    length = len_ref[0]
-    tri = jnp.where(
-        lax.broadcasted_iota(I32, (seq, seq), 0) <= lane_iota((seq, seq)), 1.0, 0.0
-    ).astype(BF)
-    eid = eid_row_ref[...]
-    live = lane_iota((1, seq)) < length
-    pick = (lax.broadcasted_iota(I32, (experts, seq), 0) == eid) & live
-    pick = jnp.where(pick, 1.0, 0.0)
-    rank = jnp.sum(dot(pick.astype(BF), tri) * pick, axis=0, keepdims=True).astype(I32) - 1
-    slot_row_ref[...] = jnp.where(live, eid * capacity + rank, experts * capacity)
-    total = experts * capacity
-    step = 4 * capacity
-
-    @pl.loop(0, total // step)
-    def _(c):
-        place(slot_row_ref, cot_ref, slots_ref, c, step)
-
-
-def collect_kernel(h_ref, slot_col_ref, ret_ref, out_ref):
-    @pl.loop(0, h_ref.shape[0] // ROWS)
-    def _(i):
-        r = rows_of(i)
-        out_ref[r, :] = h_ref[r, :] + collect(slot_col_ref, ret_ref, r)
 
 
 def flip(v, j, size):
@@ -239,9 +286,9 @@
 def expert_kernel(
     experts, capacity,
     x_ref, g_ref, win_hbm, wback_hbm,
-    ing_ref, ffn_ref, wing_ref, wbg_ref,
+    ing_ref, ffn_ref, ffn_got, wing_ref, wbg_ref,
     xin, gin, win, wback, hidden, act, ing_out, xt, own_in, own_back, got_in, got_back,
-    x_send, x_recv, r_send, r_recv, g_sem, w_sem, own_sem, ffn_sem, t_send, t_recv, o_sem,
+    x_send, x_recv, r_send, r_recv, f_send, f_recv, g_sem, w_sem, own_sem, ffn_sem, t_send, t_recv, o_sem,
 ):
     me = lax.axis_index("expert")
     other = 1 - lax.axis_index("dp")
@@ -266,8 +313,7 @@
             device_id={"expert": flip(me, j, experts)}, device_id_type=MESH,
         )
 
-    def g_copy(j):
-        return pltpu.make_async_copy(g_ref.at[block(flip(me, j, experts))], gin.at[block(j)], g_sem.at[j])
+    load_g = pltpu.make_async_copy(g_ref, gin, g_sem)
 
     own_x = pltpu.make_async_copy(x_ref.at[block(me)], xin.at[block(0)], own_sem.at[0])
     own_ing = pltpu.make_async_copy(ing_out.at[block(0)], ing_ref.at[block(me)], own_sem.at[1])
@@ -277,9 +323,7 @@
     load_in.start()
     load_back.start()
 
-    @pl.loop(0, experts)
-    def _(j):
-        g_copy(j).start()
+    load_g.start()
 
     greet(experts, True)
     for low, high in ((2, 3), (0, 2), (3, 4)):
@@ -292,13 +336,20 @@
     load_in.wait()
     load_back.wait()
 
-    @pl.loop(0, experts)
-    def _(j):
-        g_copy(j).wait()
+    load_g.wait()
 
     def ffn_copy(j):
         peer = flip(me, j, experts)
         return pltpu.make_async_copy(xin.at[block(j)], ffn_ref.at[block(peer)], ffn_sem.at[j])
+
+    def ffn_near(j):
+        return pltpu.make_async_remote_copy(
+            src_ref=xin.at[block(j)], dst_ref=ffn_got.at[block(me)],
+            send_sem=f_send.at[j], recv_sem=f_recv.at[j],
+            device_id={"expert": flip(me, j, experts)}, device_id_type=MESH,
+        )
+
+    own_ffn = pltpu.make_async_copy(xin.at[block(0)], ffn_got.at[block(me)], own_sem.at[0])
 
     @pl.loop(0, groups)
     def _(i):
@@ -343,7 +394,19 @@
             xin[r, c] = dot(hidden[r, :], wback[:, c]).astype(BF)
 
         for c in range(4):
-            ffn_copy(4 * i + c).start()
+            j = 4 * i + c
+
+            @pl.when(j >= experts // 2)
+            def _():
+                ffn_copy(j).start()
+
+            @pl.when((j > 0) & (j < experts // 2))
+            def _():
+                ffn_near(j).start()
+
+        @pl.when(i == 0)
+        def _():
+            own_ffn.start()
 
     tiles = ff // 256
 
@@ -394,14 +457,62 @@
             copy.wait()
     own_ing.wait()
 
-    @pl.loop(0, experts)
+    own_ffn.wait()
+
+    @pl.loop(experts // 2, experts)
     def _(j):
         ffn_copy(j).wait()
+
+    @pl.loop(1, experts // 2)
+    def _(j):
+        ffn_near(j).wait()
 
     @pl.loop(1, experts)
     def _(j):
         x_copy(j).wait_send()
         r_copy(j).wait()
+
+
+def forward_call(experts, capacity, lengths, eid_row, eid_col, g1, g2, x, g, w_qkv, w_out):
+    seq, width = x.shape
+    pairs, total = width // LANES, experts * capacity
+    dma = pltpu.SemaphoreType.DMA
+    vmem = pltpu.VMEM
+    return pl.pallas_call(
+        functools.partial(forward_kernel, experts, capacity),
+        out_shape=(
+            sds((seq, width), BF),
+            sds((3 * pairs, seq, LANES), BF),
+            sds((seq, width), BF),
+            sds((pairs, seq, LANES), BF),
+            sds((seq, width), F32),
+            sds((total, width), BF),
+            sds((seq, 1), I32),
+            sds((total, width), BF),
+        ),
+        in_specs=[SMEM] + [VMEM] * 4 + [ANY] * 4,
+        out_specs=(ANY,) * 6 + (VMEM, ANY),
+        scratch_shapes=[
+            vmem((seq, width), BF),
+            vmem((seq, width), BF),
+            vmem((width, 3 * width), BF),
+            vmem((width, width), BF),
+            vmem((seq, width), BF),
+            vmem((3 * pairs, seq, LANES), BF),
+            vmem((seq, width), BF),
+            vmem((pairs, seq, LANES), BF),
+            vmem((seq, width), F32),
+            vmem((total, width), BF),
+            vmem((seq, LANES), BF),
+            vmem((seq, width), BF),
+            vmem((1, seq), I32),
+            vmem((total, width), BF),
+            dma((4,)), dma((6,)), dma, dma((experts,)), dma((experts,)),
+        ],
+        compiler_params=params(60, collective_id=4, has_side_effects=True),
+        cost_estimate=pl.CostEstimate(flops=40 * 10**9, bytes_accessed=24 * 10**6, transcendentals=0),
+        name="attention_forward",
+    )(lengths, eid_row, eid_col, g1, g2, x, g, w_qkv, w_out)
 
 
 def experts_call(experts, capacity, x_slots, g_slots, w_in, w_back):
@@ -412,10 +523,11 @@
     return pl.pallas_call(
         functools.partial(expert_kernel, experts, capacity),
         out_shape=(
-            sds((total, width), BF), sds((total, width), BF), sds((width, ff), BF), sds((ff, width), BF),
+            sds((total, width), BF), sds((total, width), BF), sds((total, width), BF),
+            sds((width, ff), BF), sds((ff, width), BF),
         ),
         in_specs=[ANY] * 4,
-        out_specs=(ANY,) * 4,
+        out_specs=(ANY,) * 5,
         scratch_shapes=[
             pltpu.VMEM((total, width), BF),
             pltpu.VMEM((total, width), BF),
@@ -430,7 +542,8 @@
             pltpu.VMEM((tiles, width, 256), BF),
             pltpu.VMEM((tiles, 256, width), BF),
             dma((experts,)), dma((experts,)), dma((experts,)), dma((experts,)),
-            dma((experts,)), dma((2,)), dma((2,)), dma((experts,)),
+            dma((experts // 2,)), dma((experts // 2,)),
+            dma, dma((2,)), dma((2,)), dma((experts,)),
             dma((2, tiles)), dma((2, tiles)), dma((2, 4)),
         ],
         compiler_params=params(61, collective_id=1, has_side_effects=True),
@@ -439,42 +552,279 @@
     )(x_slots, g_slots, w_in, w_back)
 
 
+def unit_plan(experts, width):
+    pairs = width // LANES
+    runs = [None] + [(p, p + 1) for p in range(0, pairs - 2, 2)] + [(p,) for p in range(pairs - pairs % 2 - 2, pairs)]
+    plan, row = [], 0
+    for run in runs:
+        tiles = pairs if run is None else 3 * len(run)
+        piece = -(-tiles * width // (2 * experts * 16)) * 16
+        plan.append((row, run, piece))
+        row += 2 * experts * piece
+    return plan, row
+
+
 def backward_kernel(
-    len_ref, tok_ref, cot_ref, normed_ref, qkv_ref, mixed_ref, laug_ref, h_ref, ret_ref, slot_col_ref,
-    wqkv_ref, wout_ref, g1_ref, g2_ref,
-    tokg_ref, wqkvg_ref, woutg_ref, g1g_ref, g2g_ref,
+    experts, capacity,
+    len_ref, g1_ref, g2_ref, tok_hbm, cot_hbm, normed_hbm, qkv_hbm, mixed_hbm, laug_hbm, h_hbm, ret_hbm, slot_col_ref,
+    wqkv_hbm, wout_hbm, ffn_hbm, got_hbm,
+    out_ref, tokg_ref, sums_ref, g2g_ref,
+    tok_ref, qkv_ref, mixed_ref, laug_ref, h_ref, ret_ref, wqkv_ref, wout_ref, ffn_ref,
     hgrad_ref, hg_ref, mg_ref, daug_ref, kaug_ref, dq_ref, qg_ref, normt_ref,
+    part, final, got_core, got_in, got_out, g2_acc,
+    load_sem, f_send, f_recv, core_send, core_recv, in_send, in_recv, out_send, out_recv, o_sem,
 ):
     seq, width = tok_ref.shape
-    blocks, pairs = seq // ROWS, width // LANES
-    g1g_ref[...] = jnp.zeros_like(g1g_ref)
-    g2g_ref[...] = jnp.zeros_like(g2g_ref)
+    blocks, pairs, total = seq // ROWS, width // LANES, experts * capacity
+    me, core = lax.axis_index("expert"), lax.axis_index("dp")
+    inner = 2 ** ((experts.bit_length() - 1) // 2)
+    outer = experts // inner
+
+    def bits_of(u):
+        bits = list(range(experts.bit_length() - 1))
+        turn = u % (len(bits) - 1)
+        order = bits[turn:-1] + bits[:turn] + bits[-1:]
+        return order[: len(bits) // 2], order[len(bits) // 2 :]
+
+    def place_in(bits):
+        return sum(me // 2**b % 2 * 2**k for k, b in enumerate(bits))
+
+    def peer_in(bits, i):
+        return flip(me, sum(i // 2**k % 2 * 2**b for k, b in enumerate(bits)), experts)
+
+    def places(u):
+        return [place_in(bits) for bits in bits_of(u)]
+
+    plan, _ = unit_plan(experts, width)
     first = lane_iota((1, LANES)) < HEAD
+
+    def block(j):
+        return pl.ds(pl.multiple_of(j * capacity, 16), capacity)
+
+    def rows(start, size):
+        return pl.ds(pl.multiple_of(start, 16), size)
+
+    def ffn_copy(j):
+        peer = flip(me, j, experts)
+        return pltpu.make_async_remote_copy(
+            src_ref=ffn_hbm.at[block(peer)], dst_ref=ffn_ref.at[block(me)],
+            send_sem=f_send.at[j], recv_sem=f_recv.at[j],
+            device_id={"expert": peer}, device_id_type=MESH,
+        )
+
+    close = pl.ds(pl.multiple_of(me // (experts // 2) * total // 2, 16), total // 2)
+    near_ffn = pltpu.make_async_copy(got_hbm.at[close], ffn_ref.at[close], load_sem.at[0])
+    loads = [
+        pltpu.make_async_copy(src, dst, load_sem.at[1 + i])
+        for i, (src, dst) in enumerate(
+            (
+                (ret_hbm, ret_ref),
+                (h_hbm, h_ref),
+                (cot_hbm, tok_ref),
+                (wout_hbm, wout_ref),
+                (mixed_hbm, mixed_ref),
+                (normed_hbm, qg_ref.at[:, :width]),
+                (qkv_hbm, qkv_ref),
+                (laug_hbm, laug_ref),
+                (wqkv_hbm, wqkv_ref),
+            )
+        )
+    ]
+    for copy in loads[:5]:
+        copy.start()
+    load_tok = pltpu.make_async_copy(tok_hbm, tok_ref, load_sem.at[10])
+    greet(experts, True)
+
+    def send_ffn(r):
+        share = experts // 16
+        for j in range(r * share, (r + 1) * share):
+            ffn_copy(experts // 2 + j).start()
+
+    send_ffn(0)
+    send_ffn(1)
+    near_ffn.start()
+    for copy in loads[5:]:
+        copy.start()
+
+    def core_copy(u, back):
+        start, _, piece = plan[u]
+        half = experts * piece
+        src = final if back else part
+        mine, theirs = start + core * half, start + (1 - core) * half
+        return pltpu.make_async_remote_copy(
+            src_ref=src.at[rows(mine if back else theirs, half)],
+            dst_ref=final.at[rows(mine, half)] if back else got_core.at[rows(start // 2, half)],
+            send_sem=core_send.at[u, back], recv_sem=core_recv.at[u, back],
+            device_id={"dp": 1 - core}, device_id_type=MESH,
+        )
+
+    def inner_copy(u, back, i):
+        start, _, piece = plan[u]
+        size = outer * piece
+        base = start + core * experts * piece
+        near = places(u)[0]
+        peer = flip(near, i, inner)
+        src, dst = (
+            (final.at[rows(base + near * size, size)], final.at[rows(base + near * size, size)])
+            if back
+            else (
+                part.at[rows(base + peer * size, size)],
+                got_in.at[i - 1, rows(start // (2 * inner), size)],
+            )
+        )
+        return pltpu.make_async_remote_copy(
+            src_ref=src, dst_ref=dst,
+            send_sem=in_send.at[u, back, i], recv_sem=in_recv.at[u, back, i],
+            device_id={"expert": peer_in(bits_of(u)[0], i)}, device_id_type=MESH,
+        )
+
+    def outer_copy(u, back, i):
+        start, _, piece = plan[u]
+        near, far = places(u)
+        base = start + core * experts * piece + near * outer * piece
+        peer = flip(far, i, outer)
+        src, dst = (
+            (final.at[rows(base + far * piece, piece)], final.at[rows(base + far * piece, piece)])
+            if back
+            else (
+                part.at[rows(base + peer * piece, piece)],
+                got_out.at[i - 1, rows(start // (2 * experts), piece)],
+            )
+        )
+        return pltpu.make_async_remote_copy(
+            src_ref=src, dst_ref=dst,
+            send_sem=out_send.at[u, back, i], recv_sem=out_recv.at[u, back, i],
+            device_id={"expert": peer_in(bits_of(u)[1], i)}, device_id_type=MESH,
+        )
+
+    def add_up(to, at, got, count, start, size, dst_at):
+        step = 16 * max(k for k in (1, 2, 3, 4, 6, 8, 9, 12) if size // 16 % k == 0)
+
+        @pl.loop(0, size // step)
+        def _(n):
+            o = n * step
+            total = part[rows(at + o, step), :].astype(F32)
+            for i in range(count):
+                got_at = got.at[rows(start + o, step)] if count == 1 else got.at[i, rows(start + o, step)]
+                total = total + got_at[...].astype(F32)
+            to[rows(dst_at + o, step), :] = total.astype(BF)
+
+    def advance(u, stage):
+        start, _, piece = plan[u]
+        base = start + core * experts * piece
+        near, far = places(u)
+        if stage == 0:
+            core_copy(u, 0).start()
+        elif stage == 1:
+            core_copy(u, 0).wait()
+            add_up(part, base, got_core, 1, start // 2, experts * piece, base)
+            for i in range(1, inner):
+                inner_copy(u, 0, i).start()
+        elif stage == 2:
+            for i in range(1, inner):
+                inner_copy(u, 0, i).wait()
+            at = base + near * outer * piece
+            add_up(part, at, got_in, inner - 1, start // (2 * inner), outer * piece, at)
+            for i in range(1, outer):
+                outer_copy(u, 0, i).start()
+        elif stage == 3:
+            for i in range(1, outer):
+                outer_copy(u, 0, i).wait()
+            at = base + (near * outer + far) * piece
+            add_up(final, at, got_out, outer - 1, start // (2 * experts), piece, at)
+            for i in range(1, outer):
+                outer_copy(u, 1, i).start()
+        elif stage == 4:
+            for i in range(1, outer):
+                outer_copy(u, 1, i).wait()
+            for i in range(1, inner):
+                inner_copy(u, 1, i).start()
+        elif stage == 5:
+            for i in range(1, inner):
+                inner_copy(u, 1, i).wait()
+            core_copy(u, 1).start()
+        else:
+            core_copy(u, 1).wait()
+            for copy in sums_copies(u):
+                copy.start()
+
+    def sums_copies(u):
+        start, run, _ = plan[u]
+        tiles = [3 * pairs + n for n in range(pairs)] if run is None else [n * pairs + p for p in run for n in range(3)]
+        return [
+            pltpu.make_async_copy(final.at[start + i * width : start + (i + 1) * width], sums_ref.at[tile], o_sem.at[tile])
+            for i, tile in enumerate(tiles)
+        ]
+
+    for copy in loads[:5]:
+        copy.wait()
+
+    g2_acc[...] = jnp.zeros_like(g2_acc)
 
     @pl.loop(0, blocks)
     def _(i):
         r = rows_of(i)
         hat, inverse = normalize(h_ref[r, :])
         ing = collect(slot_col_ref, ret_ref, r)
-        g2g_ref[...] += jnp.sum(ing * hat, axis=0, keepdims=True)
-        grad = cot_ref[r, :].astype(F32) + norm_back(ing * g2_ref[...], hat, inverse)
+        g2_acc[...] += jnp.sum((ing * hat).reshape(ROWS // 8, 8, width), axis=0)
+        grad = tok_ref[r, :].astype(F32) + norm_back(ing * g2_ref[...], hat, inverse)
         hgrad_ref[r, :] = grad
         low = grad.astype(BF)
         hg_ref[r, :] = low
         mg = dot_t(low, wout_ref[...]).astype(BF)
+
+        @pl.when(i == blocks // 2)
+        def _():
+            send_ffn(2)
+
         for p in range(pairs):
-            part = mg[:, p * LANES : (p + 1) * LANES]
-            mg_ref[p, r, :] = part
-            prod = part.astype(F32) * mixed_ref[r, p * LANES : (p + 1) * LANES].astype(F32)
+            piece = mg[:, p * LANES : (p + 1) * LANES]
+            mg_ref[p, r, :] = piece
+            prod = piece.astype(F32) * mixed_ref[r, p * LANES : (p + 1) * LANES].astype(F32)
             zero = jnp.zeros_like(prod)
             d0 = jnp.sum(jnp.where(first, prod, zero), axis=1, keepdims=True)
             d1 = jnp.sum(jnp.where(first, zero, prod), axis=1, keepdims=True)
             daug_ref[p, r, :] = aug_of(jnp.where(first, d1, d0), 0.0)
-        normt_ref[:, r] = normed_ref[r, :].T
-
-    woutg_ref[...] = tdot(mixed_ref[...], hg_ref[...]).astype(BF)
+
+    load_tok.start()
+
+    for u, (start, run, piece) in enumerate(plan):
+        tiles = pairs if run is None else 3 * len(run)
+        spare = 2 * experts * piece - tiles * width
+        if spare:
+            part[start + tiles * width : start + tiles * width + spare, :] = jnp.zeros((spare, LANES), BF)
+            gain_at = start + tiles * width
+    for p in range(pairs):
+        gain = jnp.sum(g2_acc[:, p * LANES : (p + 1) * LANES], axis=0, keepdims=True)
+        part[gain_at + 16 * p : gain_at + 16 * p + 1, :] = gain.astype(BF)
+
+    @pl.loop(0, width // 256)
+    def _(n):
+        out = tdot(mixed_ref[...], hg_ref[:, rows_of(n, 256)]).astype(BF)
+        at = plan[0][0] + 2 * n * width
+        part[rows(at, width), :] = out[:, :LANES]
+        part[rows(at + width, width), :] = out[:, LANES:]
+
+    send_ffn(3)
+    advance(0, 0)
+    loads[5].wait()
+
+    @pl.loop(0, blocks)
+    def _(i):
+        r = rows_of(i)
+        normt_ref[:, r] = qg_ref[r, :width].T
+
     kaug_ref[...] = key_aug(seq, len_ref[0])
     scale = jnp.asarray(HEAD**-0.5, BF)
+    for copy in loads[6:]:
+        copy.wait()
+
+    ends = {}
+    for u, (_, run, _) in enumerate(plan):
+        ready = -1 if run is None else run[-1]
+        for stage, late in enumerate(LAGS[u]):
+            if ready + late >= 0:
+                ends.setdefault(ready + late, []).append((u, stage))
 
     @pl.loop(0, pairs)
     def _(p):
@@ -509,18 +859,179 @@
             dq_ref[qr, :] += tdot(jnp.concatenate(dss, axis=0), jnp.concatenate(kms, axis=0))
         qg_ref[:, rows_of(p, LANES)] = (dq_ref[...] * HEAD**-0.5).astype(BF)
 
-    @pl.loop(0, 3 * pairs // 2)
-    def _(j):
-        c = rows_of(j, 2 * LANES)
-        wqkvg_ref[:, c] = dot(normt_ref[...], qg_ref[:, c]).astype(BF)
-
-    @pl.loop(0, blocks)
-    def _(i):
+        tiles3 = [qg_ref[:, rows_of(n * pairs + p, LANES)] for n in range(3)]
+        out = dot(normt_ref[...], jnp.concatenate(tiles3, axis=1)).astype(BF)
+        for u, (start, run, _) in enumerate(plan):
+            if run is not None:
+
+                @pl.when((p >= run[0]) & (p <= run[-1]))
+                def _():
+                    for n in range(3):
+                        at = start + ((p - run[0]) * 3 + n) * width
+                        part[rows(at, width), :] = out[:, n * LANES : (n + 1) * LANES]
+
+        for at in range(pairs):
+
+            @pl.when(p == at)
+            def _():
+                if at < 4:
+                    send_ffn(4 + at)
+                for u, stage in ends.get(at, ()):
+                    advance(u, stage)
+
+    load_tok.wait()
+
+    def finish_tokens(i):
         r = rows_of(i)
         n1 = dot_t(qg_ref[r, :], wqkv_ref[...])
         hat, inverse = normalize(tok_ref[r, :].astype(F32))
-        g1g_ref[...] += jnp.sum(n1 * hat, axis=0, keepdims=True)
-        tokg_ref[r, :] = hgrad_ref[r, :] + norm_back(n1 * g1_ref[...], hat, inverse)
+        hgrad_ref[r, :] = hgrad_ref[r, :] + norm_back(n1 * g1_ref[...], hat, inverse)
+        tokg_copy(i).start()
+
+    def tokg_copy(i):
+        return pltpu.make_async_copy(hgrad_ref.at[rows_of(i)], tokg_ref.at[rows_of(i)], load_sem.at[1 + i])
+
+    def finish_output(i):
+        r = rows_of(i)
+        h_ref[r, :] = h_ref[r, :] + collect(slot_col_ref, ffn_ref, r)
+        out_copy(i).start()
+
+    def out_copy(i):
+        return pltpu.make_async_copy(h_ref.at[rows_of(i)], out_ref.at[rows_of(i)], load_sem.at[1 + blocks + i])
+
+    last = max(ends)
+    for step in range(pairs, last + 1):
+        n = step - pairs
+        if n < blocks:
+            finish_tokens(n)
+        elif n == blocks:
+            near_ffn.wait()
+
+            @pl.loop(experts // 2, experts)
+            def _(j):
+                ffn_copy(j).wait()
+
+            for i in range(blocks // 2):
+                finish_output(i)
+        elif n == blocks + 1:
+            for i in range(blocks // 2, blocks):
+                finish_output(i)
+        for u, stage in ends.get(step, ()):
+            advance(u, stage)
+
+    for p in range(pairs):
+        g2g_ref[:, p * LANES : (p + 1) * LANES] = final[gain_at + 16 * p : gain_at + 16 * p + 1, :].astype(F32)
+    for i in range(blocks):
+        tokg_copy(i).wait()
+        out_copy(i).wait()
+    for u in range(len(plan)):
+        for copy in sums_copies(u):
+            copy.wait()
+
+
+def backward_call(experts, capacity, lengths, g1, g2, x, g, normed, qkv, mixed, laug, h, ret, slot_col, w_qkv, w_out, ffn, got):
+    seq, width = x.shape
+    pairs, total = width // LANES, experts * capacity
+    plan, height = unit_plan(experts, width)
+    inner = 2 ** ((experts.bit_length() - 1) // 2)
+    outer, units = experts // inner, len(plan)
+    dma = pltpu.SemaphoreType.DMA
+    vmem = pltpu.VMEM
+    return pl.pallas_call(
+        functools.partial(backward_kernel, experts, capacity),
+        out_shape=(
+            sds((seq, width), F32), sds((seq, width), F32), sds((4 * pairs, width, LANES), BF), sds((1, width), F32),
+        ),
+        in_specs=[SMEM, VMEM, VMEM] + [ANY] * 8 + [VMEM] + [ANY] * 4,
+        out_specs=(ANY, ANY, ANY, VMEM),
+        scratch_shapes=[
+            vmem((seq, width), BF),
+            vmem((3 * pairs, seq, LANES), BF),
+            vmem((seq, width), BF),
+            vmem((pairs, seq, LANES), BF),
+            vmem((seq, width), F32),
+            vmem((total, width), BF),
+            vmem((width, 3 * width), BF),
+            vmem((width, width), BF),
+            vmem((total, width), BF),
+            vmem((seq, width), F32),
+            vmem((seq, width), BF),
+            vmem((pairs, seq, LANES), BF),
+            vmem((pairs, seq, LANES), BF),
+            vmem((seq, LANES), BF),
+            vmem((seq, LANES), F32),
+            vmem((seq, 3 * width), BF),
+            vmem((width, seq), BF),
+            vmem((height, LANES), BF),
+            vmem((height, LANES), BF),
+            vmem((height // 2, LANES), BF),
+            vmem((inner - 1, height // (2 * inner), LANES), BF),
+            vmem((outer - 1, height // (2 * experts), LANES), BF),
+            vmem((8, width), F32),
+            dma((11,)), dma((experts,)), dma((experts,)),
+            dma((units, 2)), dma((units, 2)),
+            dma((units, 2, inner)), dma((units, 2, inner)),
+            dma((units, 2, outer)), dma((units, 2, outer)),
+            dma((4 * pairs,)),
+        ],
+        compiler_params=params(62, collective_id=2, has_side_effects=True),
+        cost_estimate=pl.CostEstimate(flops=60 * 10**9, bytes_accessed=24 * 10**6, transcendentals=0),
+        name="attention_backward",
+    )(lengths, g1, g2, x, g, normed, qkv, mixed, laug, h, ret, slot_col, w_qkv, w_out, ffn, got)
+
+
+def finish_kernel(
+    win_ref, wback_ref, sums_ref, wqkv_ref, g1_ref,
+    win_out, wback_out, wqkv_out, wout_out, g1g_ref,
+    gain_ref,
+):
+    i = pl.program_id(0)
+    size = wqkv_ref.shape[0]
+    tiles = sums_ref.shape[0]
+    pairs = tiles // 4
+    win_out[...] = win_ref[...].astype(F32)
+    wback_out[...] = wback_ref[...].astype(F32)
+    gain = jnp.zeros((size, LANES), F32)
+    for t in range(tiles):
+        tile = sums_ref[t].astype(F32)
+        if t < 3 * pairs:
+            c = slice(t * LANES, (t + 1) * LANES)
+            wqkv_out[:, c] = tile
+            gain = gain + tile * wqkv_ref[:, c].astype(F32)
+        else:
+            wout_out[:, (t - 3 * pairs) * LANES : (t - 3 * pairs + 1) * LANES] = tile
+    gain_ref[rows_of(i, size), :] = gain
+
+    @pl.when(i == pl.num_programs(0) - 1)
+    def _():
+        total = lax.dot_general(
+            jnp.ones((8, LANES), F32), gain_ref[...], (((1,), (1,)), ((), ())),
+            precision=lax.Precision.HIGHEST, preferred_element_type=F32,
+        )
+        g1g_ref[...] = total[:1, :] / g1_ref[...]
+
+
+def finish_call(win, wback, sums, w_qkv, g1):
+    width, ff = win.shape
+    tiles, steps = sums.shape[0], 8
+    wide = pl.BlockSpec((width // steps, ff), lambda i: (i, 0))
+    tall = pl.BlockSpec((ff // steps, width), lambda i: (i, 0))
+    three = pl.BlockSpec((width // steps, 3 * width), lambda i: (i, 0))
+    square = pl.BlockSpec((width // steps, width), lambda i: (i, 0))
+    row = pl.BlockSpec((1, width), lambda i: (0, 0))
+    return pl.pallas_call(
+        finish_kernel,
+        grid=(steps,),
+        out_shape=(
+            sds((width, ff), F32), sds((ff, width), F32), sds((width, 3 * width), F32), sds((width, width), F32),
+            sds((1, width), F32),
+        ),
+        in_specs=[wide, tall, pl.BlockSpec((tiles, width // steps, LANES), lambda i: (0, i, 0)), three, row],
+        out_specs=(wide, tall, three, square, row),
+        scratch_shapes=[pltpu.VMEM((width, LANES), F32)],
+        compiler_params=params(61),
+        name="finish_gradients",
+    )(win, wback, sums, w_qkv, g1)
 
 
 def params(mib, **kw):
@@ -542,91 +1053,17 @@
     eid_col = expert_ids[0]
     g1, g2 = norm1_gain.reshape(1, width), norm2_gain.reshape(1, width)
 
-    g_slots, _ = pl.pallas_call(
-        functools.partial(place_kernel, experts, capacity),
-        out_shape=(sds((total, width), BF), sds((1, seq), I32)),
-        in_specs=[SMEM, VMEM, VMEM],
-        out_specs=(VMEM, VMEM),
-        compiler_params=params(40),
-        name="place_gradient",
-    )(lengths, eid_row, g)
-    g_in = exchange(g_slots, experts)
-
-    normed, qkv, mixed, laug, h, x_slots, slot_col = pl.pallas_call(
-        functools.partial(forward_kernel, experts, capacity),
-        out_shape=(
-            sds((seq, width), BF),
-            sds((3 * pairs, seq, LANES), BF),
-            sds((seq, width), BF),
-            sds((pairs, seq, LANES), BF),
-            sds((seq, width), F32),
-            sds((total, width), BF),
-            sds((seq, 1), I32),
-        ),
-        in_specs=[SMEM] + [VMEM] * 7,
-        out_specs=(VMEM,) * 7,
-        scratch_shapes=[
-            pltpu.VMEM((seq, LANES), BF),
-            pltpu.VMEM((seq, width), BF),
-            pltpu.VMEM((1, seq), I32),
-        ],
-        compiler_params=params(58),
-        cost_estimate=pl.CostEstimate(flops=40 * 10**9, bytes_accessed=24 * 10**6, transcendentals=0),
-        name="attention_forward",
-    )(lengths, x, eid_row, eid_col, w_qkv, w_out, g1, g2)
-    ing_ret, ffn, wing, wbg = experts_call(experts, capacity, x_slots, g_in, w_in[0], w_back[0])
-    ffn_ret = exchange(ffn, experts)
-
-    tokg, wqkvg, woutg, g1g, g2g = pl.pallas_call(
-        backward_kernel,
-        out_shape=(
-            sds((seq, width), F32),
-            sds((width, 3 * width), BF),
-            sds((width, width), BF),
-            sds((1, width), F32),
-            sds((1, width), F32),
-        ),
-        in_specs=[SMEM] + [VMEM] * 13,
-        out_specs=(VMEM,) * 5,
-        scratch_shapes=[
-            pltpu.VMEM((seq, width), F32),
-            pltpu.VMEM((seq, width), BF),
-            pltpu.VMEM((pairs, seq, LANES), BF),
-            pltpu.VMEM((pairs, seq, LANES), BF),
-            pltpu.VMEM((seq, LANES), BF),
-            pltpu.VMEM((seq, LANES), F32),
-            pltpu.VMEM((seq, 3 * width), BF),
-            pltpu.VMEM((width, seq), BF),
-        ],
-        compiler_params=params(60),
-        cost_estimate=pl.CostEstimate(flops=60 * 10**9, bytes_accessed=24 * 10**6, transcendentals=0),
-        name="attention_backward",
-    )(lengths, x, g, normed, qkv, mixed, laug, h, ing_ret, slot_col, w_qkv, w_out, g1, g2)
-
-    output = pl.pallas_call(
-        collect_kernel,
-        out_shape=sds((seq, width), F32),
-        in_specs=[VMEM] * 3,
-        out_specs=VMEM,
-        compiler_params=params(40),
-        name="collect_output",
-    )(h, slot_col, ffn_ret)
-
-    in_sum = wing.astype(F32)
-    back_sum = wbg.astype(F32)
-    both = ("dp", "expert")
-    out_sum = lax.psum(woutg, both).astype(F32)
-    qkv_sum = lax.psum(wqkvg, both).astype(F32)
-    g1_sum, g2_sum = lax.psum((g1g[0], g2g[0]), both)
+    normed, qkv, mixed, laug, h, x_slots, slot_col, g_in = forward_call(
+        experts, capacity, lengths, eid_row, eid_col, g1, g2, x, g, w_qkv, w_out
+    )
+    ing_ret, ffn, got, wing, wbg = experts_call(experts, capacity, x_slots, g_in, w_in[0], w_back[0])
+    output, tokg, sums, g2_sum = backward_call(
+        experts, capacity, lengths, g1, g2, x, g, normed, qkv, mixed, laug, h, ing_ret, slot_col, w_qkv, w_out, ffn, got
+    )
+    in_sum, back_sum, qkv_sum, out_sum, g1_sum = finish_call(wing, wbg, sums, w_qkv, g1)
     return (
-        output[None], tokg[None], qkv_sum, out_sum, g1_sum, g2_sum, in_sum[None], back_sum[None],
+        output[None], tokg[None], qkv_sum, out_sum, g1_sum[0], g2_sum[0], in_sum[None], back_sum[None],
     )
-
-
-def exchange(rows, experts):
-    total, width = rows.shape
-    rows = rows.reshape(experts, total // experts, width)
-    return lax.all_to_all(rows, "expert", split_axis=0, concat_axis=0, tiled=True).reshape(total, width)
 
 
 def solution(mesh):

time: 421 us -> 328 us (0.78)
  Pallas kernels: 208 us -> 315 us
  waiting for transfers between devices: 94.9 us -> 0 us
  blocking collectives: 41.2 us -> 0 us
  starting transfers between devices: 33.3 us -> 0 us
  other arithmetic: 20.8 us -> 1.89 us
  between operations: 14.8 us -> 1.32 us
    pallas_call x4 -> x3, Pallas kernels: 103 us -> 197 us  [the longest x1 128 us: backward_call(): pl.pallas_call(functools.partial(backward_kernel, experts, capacity), out...]
    psum x1 -> x0, waiting for transfers between devices: 90.5 us -> none  [shards(): qkv_sum = lax.psum(wqkvg, both).astype(F32)]
    psum x1 -> x0, blocking collectives: 41.2 us -> none  [shards(): g1_sum, g2_sum = lax.psum((g1g[0], g2g[0]), both)]
    all_to_all x2 -> x0, starting transfers between devices: 33.1 us -> none  [exchange(): lax.all_to_all(rows, 'expert', split_axis=0, concat_axis=0, tiled=True)]
    broadcast_in_dim x2 -> x0, other arithmetic: 14.3 us -> none  [the longest x1 7.4 us: shards(): in_sum[None]]
    pallas_call x1, Pallas kernels: 104 us -> 118 us  [experts_call(): pl.pallas_call(functools.partial(expert_kernel, experts, capacity), out_s...]
    convert_element_type x2 -> x0, other arithmetic: 6.47 us -> none  [the longest x1 3.48 us: shards(): qkv_sum = lax.psum(wqkvg, both).astype(F32)]
    all_to_all x2 -> x0, waiting for transfers between devices: 4.35 us -> none  [exchange(): lax.all_to_all(rows, 'expert', split_axis=0, concat_axis=0, tiled=True)]
  transfers between devices with their start and end apart: 3 -> 0, of which waited for: 2 -> 0; matrix products, arithmetic and copies ran while one was open for 5% -> 0% of each run, Pallas kernels for 22% -> 0%
where the time goes in v3:
time: 328 us
  Pallas kernels  315 us (96%)
  local copies, waits for them, and re-layouts  9.82 us (3%)
    pallas_call x1, Pallas kernels, backward_call(): pl.pallas_call(functools.partial(backward_kernel, experts, capacity), out...  128 us
    pallas_call x1, Pallas kernels, experts_call(): pl.pallas_call(functools.partial(expert_kernel, experts, capacity), out_s...  118 us
    pallas_call x1, Pallas kernels, forward_call(): pl.pallas_call(functools.partial(forward_kernel, experts, capacity), out_...  51.9 us
    pallas_call x1, Pallas kernels, finish_call(): pl.pallas_call(finish_kernel, grid=(steps,), out_shape=(sds((width, ff),...  17.2 us

profile of v3, /device:TPU:0, one launch (start us, length us, event | category | flops | bytes accessed | tf_op | source)
XLA Modules:
  0.0 327.6 jit_solution(10054971927440273198)
XLA Ops:
  0.6 1.3 reshape.25.g1_ref
  1.9 1.3 reshape.26.g2_ref
  3.8 1.7 copy.18.eid_col_ref
  5.5 51.9 %attention_forward.1 = (bf16[1024,768]{1,0:T(8,128)(2,1)}, bf16[18,1024,128]{2,1,0:T(8,128)(2,1)}, bf16[1024,768]{1,0:T(8,128)(2,1)}, bf16[6,1024,128]{2,1,0:T(8...) custom-call(s32[1]{0:T(128)S(6)} %copy.21.len_ref, ...), custom_call_target="tpu_custom_call" | custom-call | flops 40000000000 | bytes 24000000 | tf_op jit(solution)/shard_map/attention_forward/pallas_call | solution.py:481
  57.5 117.8 %experts.1 = (bf16[1536,768]{1,0:T(8,128)(2,1)}, bf16[1536,768]{1,0:T(8,128)(2,1)}, bf16[1536,768]{1,0:T(8,128)(2,1)}, bf16[768,3072]{1,0:T(8,128)(2,1)}, bf16[3072,768]{1,0:T(8,128)(2,1)}) custom-call(bf16[1536,768]{1,0:T(8,128)(2,1)} %get-tuple-element.35.x_ref, bf16[1536,768]{1,0:T(8,128)(2,1)} %get-tuple-element.36.g_ref, bf16[768,3072]{1,0:T(8,128)(2,1)} %bitcast.16, ...), custom_call_target="tpu_custom_call" | custom-call | flops 44000002048 | bytes 30000000 | tf_op jit(solution)/shard_map/experts/pallas_call | solution.py:523
  175.2 127.7 %attention_backward.1 = (f32[1024,768]{1,0:T(8,128)}, f32[1024,768]{1,0:T(8,128)}, bf16[24,768,128]{2,1,0:T(8,128)(2,1)}, f32[1,768]{1,0:T(1,128)}) custom-call(s32[1]{0:T(128)S(6)} %copy.21.len_ref, f32[1,768]{1,0:T(1,128)} %reshape.25.g1_ref, f32[1,768]{1,0:T(1,128)} %reshape.26.g2_ref, bf16[1024,768]{1,0:T(8,128)(2,1)} %bitcast.19, ...), custom_call_target="tpu_custom_call" | custom-call | flops 60000002048 | bytes 24000000 | tf_op jit(solution)/shard_map/attention_backward/pallas_call | solution.py:940
  302.9 0.0 copy-start.1
  303.0 17.2 %finish_gradients.1 = (f32[768,3072]{1,0:T(8,128)}, f32[3072,768]{1,0:T(8,128)}, f32[768,2304]{1,0:T(8,128)}, f32[768,768]{1,0:T(8,128)}, f32[1,768]{1,0:T(1,128)}) custom-call(bf16[768,3072]{1,0:T(8,128)(2,1)} %get-tuple-element.43.win_ref, bf16[3072,768]{1,0:T(8,128)(2,1)} %get-tuple-element.44.wback_ref, ...), custom_call_target="tpu_custom_call" | custom-call | tf_op jit(solution)/shard_map/finish_gradients/pallas_call | solution.py:1022
  320.2 1.3 reduce
  321.5 0.0 copy-done.1
  321.5 0.6 reduce.1
  322.1 0.0 copy-start
  322.1 3.9 %copy.22 = f32[1,1024,768]{2,1,0:T(8,128)} copy(f32[1,1024,768]{2,1,0:T(8,128)} %bitcast.11) | data formatting | bytes 6291456
  326.0 0.0 copy-done
  326.0 1.7 copy.23
Async XLA Ops:
  302.9 18.5 %copy-start.1 = (f32[1,768]{1,0:T(1,128)S(1)}, f32[1,768]{1,0:T(1,128)}, u32[]{:S(2)}) copy-start(f32[1,768]{1,0:T(1,128)} %get-tuple-element.49) | copy-start | bytes 9220
  322.1 3.9 %copy-start = (f32[1024,768]{1,0:T(8,128)S(1)}, f32[1024,768]{1,0:T(8,128)}, u32[]{:S(2)}) copy-start(f32[1024,768]{1,0:T(8,128)} %get-tuple-element.42) | copy-start | bytes 9437188

commit v4 on v3

--- a/solution.py
+++ b/solution.py
@@ -12,7 +12,8 @@
 LANES = 128
 ROWS = 256
 EPS = 1e-5
-LAGS = ((0, 1, 3, 4, 5, 7, 8), (0, 1, 3, 4, 5, 7, 8), (0, 1, 3, 4, 5, 6, 7), (0, 1, 2, 3, 4, 5, 6), (0, 1, 2, 3, 4, 5, 6))
+INNER = 8
+STAGES = ((-1, 0, 1, 2, 4, 5, 6, 7), (0, 1, 2, 3, 5, 6, 7, 8), (1, 2, 3, 4, 6, 7, 8, 9), (2, 3, 4, 5, 6, 7, 8, 9), (3, 4, 5, 6, 7, 8, 9, 10), (4, 5, 6, 7, 8, 9, 10, 11), (5, 6, 7, 8, 9, 10, 11, 12))
 NEG = -1e30
 VMEM = pl.BlockSpec(memory_space=pltpu.VMEM)
 ANY = pl.BlockSpec(memory_space=pl.ANY)
@@ -85,7 +86,7 @@
 
 def forward_kernel(
     experts, capacity,
-    len_ref, eid_row_ref, eid_col_ref, g1_ref, g2_ref, tok_hbm, cot_hbm, wqkv_hbm, wout_hbm,
+    len_ref, eid_row_ref, g1_ref, g2_ref, tok_hbm, cot_hbm, wqkv_hbm, wout_hbm,
     normed_out, qkv_out, mixed_out, laug_out, h_out, slots_out, slot_col_ref, g_got,
     tok_ref, cot_ref, wqkv_ref, wout_ref, normed_ref, qkv_ref, mixed_ref, laug_ref, h_ref, slots_ref,
     kaug_ref, xin_ref, slot_row_ref, gs_ref,
@@ -166,7 +167,7 @@
     @pl.loop(0, blocks)
     def _(i):
         hat, _ = normalize(tok_ref[rows_of(i), :].astype(F32))
-        normed_ref[rows_of(i), :] = (hat * g1_ref[...]).astype(BF)
+        normed_ref[rows_of(i), :] = (hat * g1_ref[...].reshape(1, width)).astype(BF)
 
     @pl.loop(0, 3 * pairs // 2)
     def _(j):
@@ -220,7 +221,7 @@
         h = tok_ref[r, :].astype(F32) + dot(mixed_ref[r, :], wout_ref[...])
         h_ref[r, :] = h
         hat, _ = normalize(h)
-        xin_ref[r, :] = (hat * g2_ref[...]).astype(BF)
+        xin_ref[r, :] = (hat * g2_ref[...].reshape(1, width)).astype(BF)
 
     h_copy.start()
 
@@ -229,12 +230,12 @@
         place(slot_row_ref, xin_ref, slots_ref, n, chunk)
 
     slots_copy.start()
-    eid = eid_col_ref[...]
+    eid = jnp.broadcast_to(eid_row_ref[...].astype(F32), (LANES, seq)).T.astype(I32)
     live = lax.broadcasted_iota(I32, (seq, 1), 0) < length
     pick = (lane_iota((seq, LANES)) == eid) & live
     pick = jnp.where(pick, 1.0, 0.0)
     rank = jnp.sum(tdot(tri, pick.astype(BF)) * pick, axis=1, keepdims=True).astype(I32) - 1
-    slot_col_ref[...] = jnp.where(live, eid * capacity + rank, experts * capacity)
+    slot_col_ref[...] = jnp.where(live, eid[:, :1] * capacity + rank, experts * capacity)
 
     own_g.wait()
     for copy in (normed_copy, qkv_copy, mixed_copy, laug_copy, h_copy, slots_copy):
@@ -473,7 +474,7 @@
         r_copy(j).wait()
 
 
-def forward_call(experts, capacity, lengths, eid_row, eid_col, g1, g2, x, g, w_qkv, w_out):
+def forward_call(experts, capacity, lengths, eid_row, g1, g2, x, g, w_qkv, w_out):
     seq, width = x.shape
     pairs, total = width // LANES, experts * capacity
     dma = pltpu.SemaphoreType.DMA
@@ -490,7 +491,7 @@
             sds((seq, 1), I32),
             sds((total, width), BF),
         ),
-        in_specs=[SMEM] + [VMEM] * 4 + [ANY] * 4,
+        in_specs=[SMEM] + [VMEM] * 3 + [ANY] * 4,
         out_specs=(ANY,) * 6 + (VMEM, ANY),
         scratch_shapes=[
             vmem((seq, width), BF),
@@ -512,7 +513,7 @@
         compiler_params=params(60, collective_id=4, has_side_effects=True),
         cost_estimate=pl.CostEstimate(flops=40 * 10**9, bytes_accessed=24 * 10**6, transcendentals=0),
         name="attention_forward",
-    )(lengths, eid_row, eid_col, g1, g2, x, g, w_qkv, w_out)
+    )(lengths, eid_row, g1, g2, x, g, w_qkv, w_out)
 
 
 def experts_call(experts, capacity, x_slots, g_slots, w_in, w_back):
@@ -552,15 +553,17 @@
     )(x_slots, g_slots, w_in, w_back)
 
 
-def unit_plan(experts, width):
+def unit_plan(width):
     pairs = width // LANES
-    runs = [None] + [(p, p + 1) for p in range(0, pairs - 2, 2)] + [(p,) for p in range(pairs - pairs % 2 - 2, pairs)]
+    third = pairs // 3
+    runs = [tuple(3 * pairs + third * n + m for m in range(third)) for n in range(3)]
+    runs += [(n * pairs + p,) for p in range(pairs) for n in range(3)]
     plan, row = [], 0
     for run in runs:
-        tiles = pairs if run is None else 3 * len(run)
-        piece = -(-tiles * width // (2 * experts * 16)) * 16
+        count = len(run) * width + (0 if plan else 16 * pairs)
+        piece = -(-count // (2 * INNER * 16)) * 16
         plan.append((row, run, piece))
-        row += 2 * experts * piece
+        row += 2 * INNER * piece
     return plan, row
 
 
@@ -571,31 +574,22 @@
     out_ref, tokg_ref, sums_ref, g2g_ref,
     tok_ref, qkv_ref, mixed_ref, laug_ref, h_ref, ret_ref, wqkv_ref, wout_ref, ffn_ref,
     hgrad_ref, hg_ref, mg_ref, daug_ref, kaug_ref, dq_ref, qg_ref, normt_ref,
-    part, final, got_core, got_in, got_out, g2_acc,
-    load_sem, f_send, f_recv, core_send, core_recv, in_send, in_recv, out_send, out_recv, o_sem,
+    part, final, got_core, got_pair, got_quad, got_out, g2_acc,
+    load_sem, f_send, f_recv, core_send, core_recv, pair_send, pair_recv, quad_send, quad_recv, out_send, out_recv, o_sem,
 ):
     seq, width = tok_ref.shape
     blocks, pairs, total = seq // ROWS, width // LANES, experts * capacity
     me, core = lax.axis_index("expert"), lax.axis_index("dp")
-    inner = 2 ** ((experts.bit_length() - 1) // 2)
-    outer = experts // inner
-
-    def bits_of(u):
-        bits = list(range(experts.bit_length() - 1))
-        turn = u % (len(bits) - 1)
-        order = bits[turn:-1] + bits[:turn] + bits[-1:]
-        return order[: len(bits) // 2], order[len(bits) // 2 :]
-
-    def place_in(bits):
-        return sum(me // 2**b % 2 * 2**k for k, b in enumerate(bits))
-
-    def peer_in(bits, i):
-        return flip(me, sum(i // 2**k % 2 * 2**b for k, b in enumerate(bits)), experts)
-
-    def places(u):
-        return [place_in(bits) for bits in bits_of(u)]
-
-    plan, _ = unit_plan(experts, width)
+    outer = experts // INNER
+    far = me // INNER
+
+    def spot(u):
+        bit = u % 3
+        low, high = [b for b in range(3) if b != bit]
+        return bit, me // 2**bit % 2, me // 2**low % 2 + 2 * (me // 2**high % 2)
+
+
+    plan, _ = unit_plan(width)
     first = lane_iota((1, LANES)) < HEAD
 
     def block(j):
@@ -648,7 +642,7 @@
 
     def core_copy(u, back):
         start, _, piece = plan[u]
-        half = experts * piece
+        half = INNER * piece
         src = final if back else part
         mine, theirs = start + core * half, start + (1 - core) * half
         return pltpu.make_async_remote_copy(
@@ -658,90 +652,88 @@
             device_id={"dp": 1 - core}, device_id_type=MESH,
         )
 
-    def inner_copy(u, back, i):
+    def pair_copy(u, back):
         start, _, piece = plan[u]
-        size = outer * piece
-        base = start + core * experts * piece
-        near = places(u)[0]
-        peer = flip(near, i, inner)
-        src, dst = (
-            (final.at[rows(base + near * size, size)], final.at[rows(base + near * size, size)])
-            if back
-            else (
-                part.at[rows(base + peer * size, size)],
-                got_in.at[i - 1, rows(start // (2 * inner), size)],
-            )
-        )
+        bit, side, _ = spot(u)
+        base = start + core * INNER * piece
+        own = final.at[rows(base + side * 4 * piece, 4 * piece)]
         return pltpu.make_async_remote_copy(
-            src_ref=src, dst_ref=dst,
-            send_sem=in_send.at[u, back, i], recv_sem=in_recv.at[u, back, i],
-            device_id={"expert": peer_in(bits_of(u)[0], i)}, device_id_type=MESH,
-        )
-
-    def outer_copy(u, back, i):
+            src_ref=own if back else part.at[rows(base + (1 - side) * 4 * piece, 4 * piece)],
+            dst_ref=own if back else got_pair.at[rows(start // 4, 4 * piece)],
+            send_sem=pair_send.at[u, back], recv_sem=pair_recv.at[u, back],
+            device_id={"expert": flip(me, 2**bit, experts)}, device_id_type=MESH,
+        )
+
+    def quad_copy(u, back, i):
         start, _, piece = plan[u]
-        near, far = places(u)
-        base = start + core * experts * piece + near * outer * piece
-        peer = flip(far, i, outer)
-        src, dst = (
-            (final.at[rows(base + far * piece, piece)], final.at[rows(base + far * piece, piece)])
-            if back
-            else (
-                part.at[rows(base + peer * piece, piece)],
-                got_out.at[i - 1, rows(start // (2 * experts), piece)],
-            )
-        )
+        bit, side, place = spot(u)
+        low, high = [b for b in range(3) if b != bit]
+        base = start + (core * INNER + side * 4) * piece
+        own = final.at[rows(base + place * piece, piece)]
         return pltpu.make_async_remote_copy(
-            src_ref=src, dst_ref=dst,
-            send_sem=out_send.at[u, back, i], recv_sem=out_recv.at[u, back, i],
-            device_id={"expert": peer_in(bits_of(u)[1], i)}, device_id_type=MESH,
-        )
-
-    def add_up(to, at, got, count, start, size, dst_at):
-        step = 16 * max(k for k in (1, 2, 3, 4, 6, 8, 9, 12) if size // 16 % k == 0)
+            src_ref=own if back else part.at[rows(base + flip(place, i, 4) * piece, piece)],
+            dst_ref=own if back else got_quad.at[i - 1, rows(start // (2 * INNER), piece)],
+            send_sem=quad_send.at[u, back, i], recv_sem=quad_recv.at[u, back, i],
+            device_id={"expert": flip(me, i % 2 * 2**low + i // 2 * 2**high, experts)}, device_id_type=MESH,
+        )
+
+    def outer_copy(u, i):
+        start, _, piece = plan[u]
+        own = got_out.at[far, rows(start // (2 * INNER), piece)]
+        return pltpu.make_async_remote_copy(
+            src_ref=own, dst_ref=own,
+            send_sem=out_send.at[u, i], recv_sem=out_recv.at[u, i],
+            device_id={"expert": flip(me, i * INNER, experts)}, device_id_type=MESH,
+        )
+
+    def add_up(to, sources, size):
+        step = 16 * max(k for k in range(1, 13) if size // 16 % k == 0)
 
         @pl.loop(0, size // step)
         def _(n):
-            o = n * step
-            total = part[rows(at + o, step), :].astype(F32)
-            for i in range(count):
-                got_at = got.at[rows(start + o, step)] if count == 1 else got.at[i, rows(start + o, step)]
-                total = total + got_at[...].astype(F32)
-            to[rows(dst_at + o, step), :] = total.astype(BF)
+            r = rows_of(n, step)
+            total = sources[0][r, :].astype(F32)
+            for source in sources[1:]:
+                total = total + source[r, :].astype(F32)
+            to[r, :] = total.astype(BF)
 
     def advance(u, stage):
         start, _, piece = plan[u]
-        base = start + core * experts * piece
-        near, far = places(u)
+        half = INNER * piece
+        _, side, place = spot(u)
+        mine = part.at[rows(start + core * half, half)]
+        quarter = part.at[rows(start + core * half + side * 4 * piece, 4 * piece)]
+        at = rows(start + core * half + (side * 4 + place) * piece, piece)
+        shared = rows(start // (2 * INNER), piece)
         if stage == 0:
             core_copy(u, 0).start()
         elif stage == 1:
             core_copy(u, 0).wait()
-            add_up(part, base, got_core, 1, start // 2, experts * piece, base)
-            for i in range(1, inner):
-                inner_copy(u, 0, i).start()
+            add_up(mine, [mine, got_core.at[rows(start // 2, half)]], half)
+            pair_copy(u, 0).start()
         elif stage == 2:
-            for i in range(1, inner):
-                inner_copy(u, 0, i).wait()
-            at = base + near * outer * piece
-            add_up(part, at, got_in, inner - 1, start // (2 * inner), outer * piece, at)
+            pair_copy(u, 0).wait()
+            add_up(quarter, [quarter, got_pair.at[rows(start // 4, 4 * piece)]], 4 * piece)
+            for i in range(1, 4):
+                quad_copy(u, 0, i).start()
+        elif stage == 3:
+            for i in range(1, 4):
+                quad_copy(u, 0, i).wait()
+            add_up(got_out.at[far, shared], [part.at[at]] + [got_quad.at[i, shared] for i in range(3)], piece)
             for i in range(1, outer):
-                outer_copy(u, 0, i).start()
-        elif stage == 3:
-            for i in range(1, outer):
-                outer_copy(u, 0, i).wait()
-            at = base + (near * outer + far) * piece
-            add_up(final, at, got_out, outer - 1, start // (2 * experts), piece, at)
-            for i in range(1, outer):
-                outer_copy(u, 1, i).start()
+                outer_copy(u, i).start()
         elif stage == 4:
             for i in range(1, outer):
-                outer_copy(u, 1, i).wait()
-            for i in range(1, inner):
-                inner_copy(u, 1, i).start()
+                outer_copy(u, i).wait()
+            add_up(final.at[at], [got_out.at[o, shared] for o in range(outer)], piece)
+            for i in range(1, 4):
+                quad_copy(u, 1, i).start()
         elif stage == 5:
-            for i in range(1, inner):
-                inner_copy(u, 1, i).wait()
+            for i in range(1, 4):
+                quad_copy(u, 1, i).wait()
+            pair_copy(u, 1).start()
+        elif stage == 6:
+            pair_copy(u, 1).wait()
             core_copy(u, 1).start()
         else:
             core_copy(u, 1).wait()
@@ -749,8 +741,7 @@
                 copy.start()
 
     def sums_copies(u):
-        start, run, _ = plan[u]
-        tiles = [3 * pairs + n for n in range(pairs)] if run is None else [n * pairs + p for p in run for n in range(3)]
+        start, tiles, _ = plan[u]
         return [
             pltpu.make_async_copy(final.at[start + i * width : start + (i + 1) * width], sums_ref.at[tile], o_sem.at[tile])
             for i, tile in enumerate(tiles)
@@ -767,7 +758,7 @@
         hat, inverse = normalize(h_ref[r, :])
         ing = collect(slot_col_ref, ret_ref, r)
         g2_acc[...] += jnp.sum((ing * hat).reshape(ROWS // 8, 8, width), axis=0)
-        grad = tok_ref[r, :].astype(F32) + norm_back(ing * g2_ref[...], hat, inverse)
+        grad = tok_ref[r, :].astype(F32) + norm_back(ing * g2_ref[...].reshape(1, width), hat, inverse)
         hgrad_ref[r, :] = grad
         low = grad.astype(BF)
         hg_ref[r, :] = low
@@ -788,12 +779,9 @@
 
     load_tok.start()
 
-    for u, (start, run, piece) in enumerate(plan):
-        tiles = pairs if run is None else 3 * len(run)
-        spare = 2 * experts * piece - tiles * width
-        if spare:
-            part[start + tiles * width : start + tiles * width + spare, :] = jnp.zeros((spare, LANES), BF)
-            gain_at = start + tiles * width
+    gain_at = len(plan[0][1]) * width
+    spare = 2 * INNER * plan[0][2] - gain_at
+    part[gain_at : gain_at + spare, :] = jnp.zeros((spare, LANES), BF)
     for p in range(pairs):
         gain = jnp.sum(g2_acc[:, p * LANES : (p + 1) * LANES], axis=0, keepdims=True)
         part[gain_at + 16 * p : gain_at + 16 * p + 1, :] = gain.astype(BF)
@@ -801,12 +789,15 @@
     @pl.loop(0, width // 256)
     def _(n):
         out = tdot(mixed_ref[...], hg_ref[:, rows_of(n, 256)]).astype(BF)
-        at = plan[0][0] + 2 * n * width
-        part[rows(at, width), :] = out[:, :LANES]
-        part[rows(at + width, width), :] = out[:, LANES:]
+        for m in range(2):
+            tile = 2 * n + m
+            third = pairs // 3
+            at = tile * width + jnp.where(tile < third, 0, spare)
+            part[rows(at, width), :] = out[:, m * LANES : (m + 1) * LANES]
 
     send_ffn(3)
-    advance(0, 0)
+    for n in range(3):
+        advance(n, 0)
     loads[5].wait()
 
     @pl.loop(0, blocks)
@@ -820,11 +811,9 @@
         copy.wait()
 
     ends = {}
-    for u, (_, run, _) in enumerate(plan):
-        ready = -1 if run is None else run[-1]
-        for stage, late in enumerate(LAGS[u]):
-            if ready + late >= 0:
-                ends.setdefault(ready + late, []).append((u, stage))
+    for unit, points in enumerate(STAGES):
+        for stage, at in enumerate(points):
+            ends.setdefault(at, []).extend((3 * unit + n, stage) for n in range(3))
 
     @pl.loop(0, pairs)
     def _(p):
@@ -861,14 +850,9 @@
 
         tiles3 = [qg_ref[:, rows_of(n * pairs + p, LANES)] for n in range(3)]
         out = dot(normt_ref[...], jnp.concatenate(tiles3, axis=1)).astype(BF)
-        for u, (start, run, _) in enumerate(plan):
-            if run is not None:
-
-                @pl.when((p >= run[0]) & (p <= run[-1]))
-                def _():
-                    for n in range(3):
-                        at = start + ((p - run[0]) * 3 + n) * width
-                        part[rows(at, width), :] = out[:, n * LANES : (n + 1) * LANES]
+        for n in range(3):
+            at = plan[3][0] + (3 * p + n) * width
+            part[rows(at, width), :] = out[:, n * LANES : (n + 1) * LANES]
 
         for at in range(pairs):
 
@@ -885,7 +869,7 @@
         r = rows_of(i)
         n1 = dot_t(qg_ref[r, :], wqkv_ref[...])
         hat, inverse = normalize(tok_ref[r, :].astype(F32))
-        hgrad_ref[r, :] = hgrad_ref[r, :] + norm_back(n1 * g1_ref[...], hat, inverse)
+        hgrad_ref[r, :] = hgrad_ref[r, :] + norm_back(n1 * g1_ref[...].reshape(1, width), hat, inverse)
         tokg_copy(i).start()
 
     def tokg_copy(i):
@@ -899,28 +883,25 @@
     def out_copy(i):
         return pltpu.make_async_copy(h_ref.at[rows_of(i)], out_ref.at[rows_of(i)], load_sem.at[1 + blocks + i])
 
-    last = max(ends)
-    for step in range(pairs, last + 1):
+    for step in range(pairs, max(ends) + 1):
+        for u, stage in ends[step]:
+            advance(u, stage)
         n = step - pairs
         if n < blocks:
             finish_tokens(n)
-        elif n == blocks:
-            near_ffn.wait()
-
-            @pl.loop(experts // 2, experts)
-            def _(j):
-                ffn_copy(j).wait()
-
-            for i in range(blocks // 2):
+        elif n < blocks + 2:
+            if n == blocks:
+                near_ffn.wait()
+
+                @pl.loop(experts // 2, experts)
+                def _(j):
+                    ffn_copy(j).wait()
+
+            for i in range((n - blocks) * blocks // 2, (n - blocks + 1) * blocks // 2):
                 finish_output(i)
-        elif n == blocks + 1:
-            for i in range(blocks // 2, blocks):
-                finish_output(i)
-        for u, stage in ends.get(step, ()):
-            advance(u, stage)
 
     for p in range(pairs):
-        g2g_ref[:, p * LANES : (p + 1) * LANES] = final[gain_at + 16 * p : gain_at + 16 * p + 1, :].astype(F32)
+        g2g_ref[p * LANES : (p + 1) * LANES] = final[gain_at + 16 * p : gain_at + 16 * p + 1, :].astype(F32).reshape(LANES)
     for i in range(blocks):
         tokg_copy(i).wait()
         out_copy(i).wait()
@@ -932,15 +913,14 @@
 def backward_call(experts, capacity, lengths, g1, g2, x, g, normed, qkv, mixed, laug, h, ret, slot_col, w_qkv, w_out, ffn, got):
     seq, width = x.shape
     pairs, total = width // LANES, experts * capacity
-    plan, height = unit_plan(experts, width)
-    inner = 2 ** ((experts.bit_length() - 1) // 2)
-    outer, units = experts // inner, len(plan)
+    plan, height = unit_plan(width)
+    outer, units = experts // INNER, len(plan)
     dma = pltpu.SemaphoreType.DMA
     vmem = pltpu.VMEM
     return pl.pallas_call(
         functools.partial(backward_kernel, experts, capacity),
         out_shape=(
-            sds((seq, width), F32), sds((seq, width), F32), sds((4 * pairs, width, LANES), BF), sds((1, width), F32),
+            sds((seq, width), F32), sds((seq, width), F32), sds((4 * pairs, width, LANES), BF), sds((width,), F32),
         ),
         in_specs=[SMEM, VMEM, VMEM] + [ANY] * 8 + [VMEM] + [ANY] * 4,
         out_specs=(ANY, ANY, ANY, VMEM),
@@ -965,13 +945,15 @@
             vmem((height, LANES), BF),
             vmem((height, LANES), BF),
             vmem((height // 2, LANES), BF),
-            vmem((inner - 1, height // (2 * inner), LANES), BF),
-            vmem((outer - 1, height // (2 * experts), LANES), BF),
+            vmem((height // 4, LANES), BF),
+            vmem((3, height // (2 * INNER), LANES), BF),
+            vmem((outer, height // (2 * INNER), LANES), BF),
             vmem((8, width), F32),
             dma((11,)), dma((experts,)), dma((experts,)),
             dma((units, 2)), dma((units, 2)),
-            dma((units, 2, inner)), dma((units, 2, inner)),
-            dma((units, 2, outer)), dma((units, 2, outer)),
+            dma((units, 2)), dma((units, 2)),
+            dma((units, 2, 4)), dma((units, 2, 4)),
+            dma((units, outer)), dma((units, outer)),
             dma((4 * pairs,)),
         ],
         compiler_params=params(62, collective_id=2, has_side_effects=True),
@@ -1008,7 +990,7 @@
             jnp.ones((8, LANES), F32), gain_ref[...], (((1,), (1,)), ((), ())),
             precision=lax.Precision.HIGHEST, preferred_element_type=F32,
         )
-        g1g_ref[...] = total[:1, :] / g1_ref[...]
+        g1g_ref[...] = (total[0] / g1_ref[...])
 
 
 def finish_call(win, wback, sums, w_qkv, g1):
@@ -1018,13 +1000,13 @@
     tall = pl.BlockSpec((ff // steps, width), lambda i: (i, 0))
     three = pl.BlockSpec((width // steps, 3 * width), lambda i: (i, 0))
     square = pl.BlockSpec((width // steps, width), lambda i: (i, 0))
-    row = pl.BlockSpec((1, width), lambda i: (0, 0))
+    row = pl.BlockSpec((width,), lambda i: (0,))
     return pl.pallas_call(
         finish_kernel,
         grid=(steps,),
         out_shape=(
             sds((width, ff), F32), sds((ff, width), F32), sds((width, 3 * width), F32), sds((width, width), F32),
-            sds((1, width), F32),
+            sds((width,), F32),
         ),
         in_specs=[wide, tall, pl.BlockSpec((tiles, width // steps, LANES), lambda i: (0, i, 0)), three, row],
         out_specs=(wide, tall, three, square, row),
@@ -1050,11 +1032,10 @@
     capacity = (capacity + 15) // 16 * 16
     total = experts * capacity
     eid_row = expert_ids.reshape(1, seq)
-    eid_col = expert_ids[0]
-    g1, g2 = norm1_gain.reshape(1, width), norm2_gain.reshape(1, width)
+    g1, g2 = norm1_gain, norm2_gain
 
     normed, qkv, mixed, laug, h, x_slots, slot_col, g_in = forward_call(
-        experts, capacity, lengths, eid_row, eid_col, g1, g2, x, g, w_qkv, w_out
+        experts, capacity, lengths, eid_row, g1, g2, x, g, w_qkv, w_out
     )
     ing_ret, ffn, got, wing, wbg = experts_call(experts, capacity, x_slots, g_in, w_in[0], w_back[0])
     output, tokg, sums, g2_sum = backward_call(
@@ -1062,7 +1043,7 @@
     )
     in_sum, back_sum, qkv_sum, out_sum, g1_sum = finish_call(wing, wbg, sums, w_qkv, g1)
     return (
-        output[None], tokg[None], qkv_sum, out_sum, g1_sum[0], g2_sum[0], in_sum[None], back_sum[None],
+        output[None], tokg[None], qkv_sum, out_sum, g1_sum, g2_sum, in_sum[None], back_sum[None],
     )
 
 

time: 328 us -> 309 us (0.942)
  Pallas kernels: 315 us -> 302 us
  local copies, waits for them, and re-layouts: 9.82 us -> 6.17 us
    pallas_call x1, Pallas kernels: 128 us -> 115 us  [backward_call(): pl.pallas_call(functools.partial(backward_kernel, experts, capacity), out...]
where the time goes in v4:
time: 309 us
  Pallas kernels  302 us (98%)
  local copies, waits for them, and re-layouts  6.17 us (2%)
    pallas_call x1, Pallas kernels, experts_call(): pl.pallas_call(functools.partial(expert_kernel, experts, capacity), out_s...  118 us
    pallas_call x1, Pallas kernels, backward_call(): pl.pallas_call(functools.partial(backward_kernel, experts, capacity), out...  115 us
    pallas_call x1, Pallas kernels, forward_call(): pl.pallas_call(functools.partial(forward_kernel, experts, capacity), out_...  51.6 us
    pallas_call x1, Pallas kernels, finish_call(): pl.pallas_call(finish_kernel, grid=(steps,), out_shape=(sds((width, ff),...  17.2 us

profile of v4, /device:TPU:0, one launch (start us, length us, event | category | flops | bytes accessed | tf_op | source)
XLA Modules:
  0.0 309.2 jit_solution(10645053497961198316)
XLA Ops:
  1.3 51.6 %attention_forward.1 = (bf16[1024,768]{1,0:T(8,128)(2,1)}, bf16[18,1024,128]{2,1,0:T(8,128)(2,1)}, bf16[1024,768]{1,0:T(8,128)(2,1)}, bf16[6,1024,128]{2,1,0:T(8...) custom-call(s32[1]{0:T(128)S(6)} %copy.21.len_ref, ...), custom_call_target="tpu_custom_call" | custom-call | flops 40000000000 | bytes 24000000 | tf_op jit(solution)/shard_map/attention_forward/pallas_call | solution.py:482
  52.9 117.8 %experts.1 = (bf16[1536,768]{1,0:T(8,128)(2,1)}, bf16[1536,768]{1,0:T(8,128)(2,1)}, bf16[1536,768]{1,0:T(8,128)(2,1)}, bf16[768,3072]{1,0:T(8,128)(2,1)}, bf16[3072,768]{1,0:T(8,128)(2,1)}) custom-call(bf16[1536,768]{1,0:T(8,128)(2,1)} %get-tuple-element.35.x_ref, bf16[1536,768]{1,0:T(8,128)(2,1)} %get-tuple-element.36.g_ref, bf16[768,3072]{1,0:T(8,128)(2,1)} %bitcast.13, ...), custom_call_target="tpu_custom_call" | custom-call | flops 44000002048 | bytes 30000000 | tf_op jit(solution)/shard_map/experts/pallas_call | solution.py:524
  170.7 115.1 %attention_backward.1 = (f32[1024,768]{1,0:T(8,128)}, f32[1024,768]{1,0:T(8,128)}, bf16[24,768,128]{2,1,0:T(8,128)(2,1)}, f32[768]{0:T(1024)}) custom-call(s32[1]{0:T(128)S(6)} %copy.21.len_ref, f32[768]{0:T(1024)} %g1_ref.5, f32[768]{0:T(1024)} %g2_ref.3, bf16[1024,768]{1,0:T(8,128)(2,1)} %bitcast.16, bf16[1024,768]{1,0:T(8,128)(2,1)} %bitcast.18, ...), custom_call_target="tpu_custom_call" | custom-call | flops 60000002048 | bytes 24000000 | tf_op jit(solution)/shard_map/attention_backward/pallas_call | solution.py:920
  285.8 17.2 %finish_gradients.1 = (f32[768,3072]{1,0:T(8,128)}, f32[3072,768]{1,0:T(8,128)}, f32[768,2304]{1,0:T(8,128)}, f32[768,768]{1,0:T(8,128)}, f32[768]{0:T(1024)}) custom-call(bf16[768,3072]{1,0:T(8,128)(2,1)} %get-tuple-element.43.win_ref, bf16[3072,768]{1,0:T(8,128)(2,1)} %get-tuple-element.44.wback_ref, bf16[24,768,128]{2,1,0:T(8,128)(2,1)} %get-tuple-element.45.sums_ref, ...), custom_call_target="tpu_custom_call" | custom-call | tf_op jit(solution)/shard_map/finish_gradients/pallas_call | solution.py:1004
  303.0 0.0 copy-start
  303.0 3.9 %copy.22 = f32[1,1024,768]{2,1,0:T(8,128)} copy(f32[1,1024,768]{2,1,0:T(8,128)} %bitcast.10) | data formatting | bytes 6291456
  306.9 0.0 copy-done
  306.9 0.0 copy-start.1
  306.9 1.7 copy.23
  308.6 0.0 copy-done.1
  308.6 0.6 copy.24
Async XLA Ops:
  303.0 3.9 %copy-start = (f32[1024,768]{1,0:T(8,128)S(1)}, f32[1024,768]{1,0:T(8,128)}, u32[]{:S(2)}) copy-start(f32[1024,768]{1,0:T(8,128)} %get-tuple-element.42) | copy-start | bytes 9437188
  306.9 1.7 copy-start.1

commit v5 on v4

--- a/solution.py
+++ b/solution.py
@@ -13,7 +13,7 @@
 ROWS = 256
 EPS = 1e-5
 INNER = 8
-STAGES = ((-1, 0, 1, 2, 4, 5, 6, 7), (0, 1, 2, 3, 5, 6, 7, 8), (1, 2, 3, 4, 6, 7, 8, 9), (2, 3, 4, 5, 6, 7, 8, 9), (3, 4, 5, 6, 7, 8, 9, 10), (4, 5, 6, 7, 8, 9, 10, 11), (5, 6, 7, 8, 9, 10, 11, 12))
+STAGES = ((-1, 0, 1, 2, 4, 5, 6, 7), (1, 2, 3, 4, 5, 6, 7, 8), (3, 4, 5, 6, 7, 8, 9, 10), (4, 5, 6, 7, 8, 9, 10, 11), (5, 6, 7, 8, 9, 10, 11, 12))
 NEG = -1e30
 VMEM = pl.BlockSpec(memory_space=pltpu.VMEM)
 ANY = pl.BlockSpec(memory_space=pl.ANY)
@@ -557,7 +557,8 @@
     pairs = width // LANES
     third = pairs // 3
     runs = [tuple(3 * pairs + third * n + m for m in range(third)) for n in range(3)]
-    runs += [(n * pairs + p,) for p in range(pairs) for n in range(3)]
+    runs += [(n * pairs + p, n * pairs + p + 1) for p in range(0, pairs - 2, 2) for n in range(3)]
+    runs += [(n * pairs + p,) for p in range(pairs - 2, pairs) for n in range(3)]
     plan, row = [], 0
     for run in runs:
         count = len(run) * width + (0 if plan else 16 * pairs)
@@ -851,7 +852,8 @@
         tiles3 = [qg_ref[:, rows_of(n * pairs + p, LANES)] for n in range(3)]
         out = dot(normt_ref[...], jnp.concatenate(tiles3, axis=1)).astype(BF)
         for n in range(3):
-            at = plan[3][0] + (3 * p + n) * width
+            early = p // 2 * 6 + n * 2 + p % 2
+            at = plan[3][0] + jnp.where(p < pairs - 2, early, 3 * p + n) * width
             part[rows(at, width), :] = out[:, n * LANES : (n + 1) * LANES]
 
         for at in range(pairs):
@@ -963,14 +965,16 @@
 
 
 def finish_kernel(
-    win_ref, wback_ref, sums_ref, wqkv_ref, g1_ref,
-    win_out, wback_out, wqkv_out, wout_out, g1g_ref,
+    win_ref, wback_ref, sums_ref, wqkv_ref, g1_ref, out_ref, tokg_ref,
+    win_out, wback_out, wqkv_out, wout_out, g1g_ref, out_out, tokg_out,
     gain_ref,
 ):
     i = pl.program_id(0)
     size = wqkv_ref.shape[0]
     tiles = sums_ref.shape[0]
     pairs = tiles // 4
+    out_out[...] = out_ref[...]
+    tokg_out[...] = tokg_ref[...]
     win_out[...] = win_ref[...].astype(F32)
     wback_out[...] = wback_ref[...].astype(F32)
     gain = jnp.zeros((size, LANES), F32)
@@ -993,7 +997,7 @@
         g1g_ref[...] = (total[0] / g1_ref[...])
 
 
-def finish_call(win, wback, sums, w_qkv, g1):
+def finish_call(win, wback, sums, w_qkv, g1, out, tokg):
     width, ff = win.shape
     tiles, steps = sums.shape[0], 8
     wide = pl.BlockSpec((width // steps, ff), lambda i: (i, 0))
@@ -1001,19 +1005,20 @@
     three = pl.BlockSpec((width // steps, 3 * width), lambda i: (i, 0))
     square = pl.BlockSpec((width // steps, width), lambda i: (i, 0))
     row = pl.BlockSpec((width,), lambda i: (0,))
+    part = pl.BlockSpec((out.shape[0] // steps, width), lambda i: (i, 0))
     return pl.pallas_call(
         finish_kernel,
         grid=(steps,),
         out_shape=(
             sds((width, ff), F32), sds((ff, width), F32), sds((width, 3 * width), F32), sds((width, width), F32),
-            sds((width,), F32),
+            sds((width,), F32), sds(out.shape, F32), sds(out.shape, F32),
         ),
-        in_specs=[wide, tall, pl.BlockSpec((tiles, width // steps, LANES), lambda i: (0, i, 0)), three, row],
-        out_specs=(wide, tall, three, square, row),
+        in_specs=[wide, tall, pl.BlockSpec((tiles, width // steps, LANES), lambda i: (0, i, 0)), three, row, part, part],
+        out_specs=(wide, tall, three, square, row, part, part),
         scratch_shapes=[pltpu.VMEM((width, LANES), F32)],
         compiler_params=params(61),
         name="finish_gradients",
-    )(win, wback, sums, w_qkv, g1)
+    )(win, wback, sums, w_qkv, g1, out, tokg)
 
 
 def params(mib, **kw):
@@ -1041,7 +1046,7 @@
     output, tokg, sums, g2_sum = backward_call(
         experts, capacity, lengths, g1, g2, x, g, normed, qkv, mixed, laug, h, ing_ret, slot_col, w_qkv, w_out, ffn, got
     )
-    in_sum, back_sum, qkv_sum, out_sum, g1_sum = finish_call(wing, wbg, sums, w_qkv, g1)
+    in_sum, back_sum, qkv_sum, out_sum, g1_sum, output, tokg = finish_call(wing, wbg, sums, w_qkv, g1, output, tokg)
     return (
         output[None], tokg[None], qkv_sum, out_sum, g1_sum, g2_sum, in_sum[None], back_sum[None],
     )

time: 309 us -> 306 us (level)
  local copies, waits for them, and re-layouts: 6.17 us -> 0.6 us
    unnamed x7 -> x3, local copies, waits for them, and re-layouts: 6.17 us -> 0.6 us
    pallas_call x1, Pallas kernels: 17.2 us -> 20.5 us  [finish_call(): pl.pallas_call(finish_kernel, grid=(steps,), out_shape=(sds((width, ff),...]
where the time goes in v5:
time: 306 us
  Pallas kernels  304 us (99%)
    pallas_call x1, Pallas kernels, experts_call(): pl.pallas_call(functools.partial(expert_kernel, experts, capacity), out_s...  118 us
    pallas_call x1, Pallas kernels, backward_call(): pl.pallas_call(functools.partial(backward_kernel, experts, capacity), out...  114 us
    pallas_call x1, Pallas kernels, forward_call(): pl.pallas_call(functools.partial(forward_kernel, experts, capacity), out_...  51.6 us
    pallas_call x1, Pallas kernels, finish_call(): pl.pallas_call(finish_kernel, grid=(steps,), out_shape=(sds((width, ff),...  20.5 us

profile of v5, /device:TPU:0, one launch (start us, length us, event | category | flops | bytes accessed | tf_op | source)
XLA Modules:
  0.0 306.1 jit_solution(539200046131577119)
XLA Ops:
  1.3 51.6 %attention_forward.1 = (bf16[1024,768]{1,0:T(8,128)(2,1)}, bf16[18,1024,128]{2,1,0:T(8,128)(2,1)}, bf16[1024,768]{1,0:T(8,128)(2,1)}, bf16[6,1024,128]{2,1,0:T(8...) custom-call(s32[1]{0:T(128)S(6)} %copy.19.len_ref, ...), custom_call_target="tpu_custom_call" | custom-call | flops 40000000000 | bytes 24000000 | tf_op jit(solution)/shard_map/attention_forward/pallas_call | solution.py:482
  52.9 117.8 %experts.1 = (bf16[1536,768]{1,0:T(8,128)(2,1)}, bf16[1536,768]{1,0:T(8,128)(2,1)}, bf16[1536,768]{1,0:T(8,128)(2,1)}, bf16[768,3072]{1,0:T(8,128)(2,1)}, bf16[3072,768]{1,0:T(8,128)(2,1)}) custom-call(bf16[1536,768]{1,0:T(8,128)(2,1)} %get-tuple-element.32.x_ref, bf16[1536,768]{1,0:T(8,128)(2,1)} %get-tuple-element.33.g_ref, bf16[768,3072]{1,0:T(8,128)(2,1)} %bitcast.11, ...), custom_call_target="tpu_custom_call" | custom-call | flops 44000002048 | bytes 30000000 | tf_op jit(solution)/shard_map/experts/pallas_call | solution.py:524
  170.7 114.2 %attention_backward.1 = (f32[1024,768]{1,0:T(8,128)}, f32[1024,768]{1,0:T(8,128)}, bf16[24,768,128]{2,1,0:T(8,128)(2,1)}, f32[768]{0:T(1024)}) custom-call(s32[1]{0:T(128)S(6)} %copy.19.len_ref, f32[768]{0:T(1024)} %g1_ref.5, f32[768]{0:T(1024)} %g2_ref.3, bf16[1024,768]{1,0:T(8,128)(2,1)} %bitcast.16, bf16[1024,768]{1,0:T(8,128)(2,1)} %bitcast.18, ...), custom_call_target="tpu_custom_call" | custom-call | flops 60000002048 | bytes 24000000 | tf_op jit(solution)/shard_map/attention_backward/pallas_call | solution.py:922
  284.9 0.0 copy-start
  284.9 20.5 %finish_gradients.1 = (f32[768,3072]{1,0:T(8,128)}, f32[3072,768]{1,0:T(8,128)}, f32[768,2304]{1,0:T(8,128)}, f32[768,768]{1,0:T(8,128)}, f32[768]{0:T(1024)}, /*index=5*/f32[1024,768]{1,0:T(8,128)}, f32[1024,768]{1,0:T(8,128)}) custom-call(bf16[768,3072]{1,0:T(8,128)(2,1)} %get-tuple-element.34.win_ref, bf16[3072,768]{1,0:T(8,128)(2,1)} %get-tuple-element.35.wback_ref, ...), custom_call_target="tpu_custom_call" | custom-call | tf_op jit(solution)/shard_map/finish_gradients/pallas_call | solution.py:1009
  305.5 0.0 copy-done
  305.5 0.6 copy.20
Async XLA Ops:
  284.9 20.5 %copy-start = (f32[768]{0:T(1024)S(1)}, f32[768]{0:T(1024)}, u32[]{:S(2)}) copy-start(f32[768]{0:T(1024)} %get-tuple-element.69) | copy-start | bytes 9220
